TPU v7x, 256 devices: a whole 4x4x8 slice. The times are simulated.
256 devices in a mesh: row: 16 (over z, y_hi), col: 8 (over y_lo, x), depth: 2 (over core).
Axes of the slice: x: 4, y: 4 (y_hi: 2, y_lo: 2; y = y_hi * 2 + y_lo), z: 8, core: 2. Of those that a mesh axis runs over, the one named last changes fastest.
Arguments:
- inputs: float32 [2048, 12288], P(('col', 'depth'), 'row'), may hold values from -0.125 to 0.125
- out_grad: float32 [2048, 12288], P('row', ('col', 'depth')), may hold values from -6 to 6
- weight: float32 [12288, 12288], P('row', ('col', 'depth')), may hold values from -0.0546875 to 0.0546875
Outputs:
- input_grad: float32 [2048, 12288], P(('col', 'depth'), 'row')
- weight_grad: float32 [12288, 12288], P('row', ('col', 'depth'))
All inputs are finite; a program needn't handle non-finite values.
Results may differ from a plain program's by a relative error of at most 0.000088.
Values sent between devices are 32-bit elements; how exact they have to be, the bound alone decides.
A program may use at most 64 MiB of HBM per device.

v0:
```python
import jax
import jax.numpy as jnp
from jax import lax
from jax.sharding import PartitionSpec as P


def contract_rows(left, right):
    return lax.dot_general(
        left,
        right,
        (((0,), (0,)), ((), ())),
        precision=lax.Precision.HIGHEST,
        preferred_element_type=jnp.float32,
    )


def contract_cols(left, right):
    return lax.dot_general(
        left,
        right,
        (((1,), (1,)), ((), ())),
        precision=lax.Precision.HIGHEST,
        preferred_element_type=jnp.float32,
    )


def local(inputs, out_grad, weight):
    input_all = lax.all_gather(inputs, ("col", "depth"), axis=0, tiled=True)
    grad_all = lax.all_gather(out_grad, "row", axis=0, tiled=True)
    weight_grad = contract_rows(input_all, grad_all)
    input_grad = lax.psum_scatter(
        contract_cols(grad_all, weight), ("col", "depth"), scatter_dimension=0, tiled=True
    )
    return (input_grad, weight_grad)


def solution(mesh):
    placed = (P(("col", "depth"), "row"), P("row", ("col", "depth")), P("row", ("col", "depth")))
    return jax.shard_map(
        local,
        mesh=mesh,
        in_specs=placed,
        out_specs=(P(("col", "depth"), "row"), P("row", ("col", "depth"))),
        check_vma=False,
    )
```

profile of v0, /device:TPU:22, one launch (start us, length us, event | category | flops | bytes accessed | tf_op | source)
XLA Modules:
  0.0 252.3 jit_solution(11024054746082631855)
XLA Ops:
  7.2 0.0 copy-start
  7.2 0.0 all-gather.3.cloned.1.call-start
  7.2 0.7 all-gather.3.cloned.1.call-update
  7.9 0.0 all-gather.5.cloned.1.call-start
  8.0 0.7 all-gather.5.cloned.1.call-update
  8.7 0.0 reduce-scatter.2.cloned.1.call-start
  8.7 118.0 %all-gather.3.cloned.1.call-done = f32[2048,768]{1,0:T(8,128)} async-done(((f32[128,768]{1,0:T(8,128)}), f32[2048,768]{1,0:T(8,128)}) %all-gather.3.cloned.1.call-update) | async-done | bytes 6291472 | tf_op jit(solution)/shard_map/all_gather | solution.py:29
  126.7 0.0 copy-done
  126.7 19.0 %fusion = f32[2048,768]{1,0:T(8,128)} fusion(f32[2048,768]{1,0:T(8,128)} %all-gather.3.cloned.1.call-done, f32[768,768]{1,0:T(8,128)S(1)} %copy-done), kind=kOutput, calls=%fused_computation | convolution fusion | flops 14495514624 | bytes 14942208 | tf_op jit(solution)/shard_map/dot_general | solution.py:18
  145.6 0.0 reduce-scatter.2.cloned.1.call-update
  145.7 26.7 %all-gather.5.cloned.1.call-done = f32[2048,768]{1,0:T(8,128)} async-done(((f32[128,768]{1,0:T(8,128)}), f32[2048,768]{1,0:T(8,128)}) %all-gather.5.cloned.1.call-update) | async-done | bytes 6291472 | tf_op jit(solution)/shard_map/all_gather | solution.py:28
  172.4 20.0 %fusion.1 = f32[768,768]{1,0:T(8,128)} fusion(f32[2048,768]{1,0:T(8,128)} %all-gather.5.cloned.1.call-done, f32[2048,768]{1,0:T(8,128)} %all-gather.3.cloned.1.call-done), kind=kOutput, calls=%fused_computation.1 | convolution fusion | flops 14495514624 | bytes 14942208 | tf_op jit(solution)/shard_map/dot_general | solution.py:8
  192.4 53.4 %reduce-scatter.2.cloned.1.call-done = f32[128,768]{1,0:T(8,128)} async-done(((f32[2048,768]{1,0:T(8,128)}), f32[128,768]{1,0:T(8,128)}) %reduce-scatter.2.cloned.1.call-update) | async-done | bytes 393232 | tf_op jit(solution)/shard_map/reduce_scatter | solution.py:31
Async XLA Ops:
  7.2 119.5 %copy-start = (f32[768,768]{1,0:T(8,128)S(1)}, f32[768,768]{1,0:T(8,128)}, u32[]{:S(2)}) copy-start(f32[768,768]{1,0:T(8,128)} %param.5) | copy-start | bytes 7077892
  7.2 119.5 %all-gather.3.cloned.1.call-start = ((), (), s32[]{:S(2)}) async-start(), calls=%async_computation.1 | async-start | bytes 6684672 | tf_op jit(solution)/shard_map/all_gather | solution.py:29
  7.9 164.4 %all-gather.5.cloned.1.call-start = ((), (), s32[]{:S(2)}) async-start(), calls=%async_computation.3 | async-start | bytes 6684672 | tf_op jit(solution)/shard_map/all_gather | solution.py:28
  8.7 237.1 %reduce-scatter.2.cloned.1.call-start = ((), (), s32[]{:S(2)}) async-start(), calls=%async_computation.2 | async-start | bytes 6684672 | tf_op jit(solution)/shard_map/reduce_scatter | solution.py:31
Sparse Core Ops, SparseCore 0:
  10.6 116.0 all-gather.2
  128.5 43.7 all-gather.4
  175.5 70.2 reduce-scatter.1
where the time goes:
time: 257 us; the launch traced here: 252 us
  waiting for transfers between devices  199 us (77%)
  matrix products  39 us (15%)
  between operations  13.8 us (5%)
    all_gather x1, waiting for transfers between devices, local(): grad_all = lax.all_gather(out_grad, 'row', axis=0, tiled=True)  118 us
    reduce_scatter x1, waiting for transfers between devices, local(): lax.psum_scatter(contract_cols(grad_all, weight), ('col', 'depth'), scatt...  53.4 us
    all_gather x1, waiting for transfers between devices, local(): input_all = lax.all_gather(inputs, ('col', 'depth'), axis=0, tiled=True)  26.7 us
    dot_general x1, matrix products, contract_rows(): lax.dot_general(left, right, (((0,), (0,)), ((), ())), precision=lax.Prec...  20 us
    dot_general x1, matrix products, contract_cols(): lax.dot_general(left, right, (((1,), (1,)), ((), ())), precision=lax.Prec...  19 us
  transfers between devices with their start and end apart: 3, of which 3 were waited for; matrix products, arithmetic and copies ran while one was open for 15% of the time, Pallas kernels for 0%

commit v1 on v0

v1 whole, which is shorter than its diff:
```python
import jax
import jax.numpy as jnp
from jax import lax
from jax.experimental import pallas as pl
from jax.experimental.pallas import tpu as pltpu
from jax.sharding import PartitionSpec as P

MESH = pl.DeviceIdType.MESH
F32 = jnp.float32
BF16 = jnp.bfloat16
N_SEM = 176
ZS = (0, 1, -1, 2, -2, 3, -3, 4)


def split(value):
    high = value.astype(BF16)
    return high, (value - high.astype(F32)).astype(BF16)


def dot3(left, right, dims):
    def one(a, b):
        return lax.dot_general(a, b, (dims, ((), ())), preferred_element_type=F32)

    return one(left[0], right[0]) + one(left[0], right[1]) + one(left[1], right[0])


def kernel(
    in_hbm, og_hbm, w_hbm, ig_hbm, wg_hbm,
    og, inp, w, w_hi, w_lo, part, from_core, from_up, from_down, from_y, wg,
    local_sem, send_sem, recv_sem,
):
    rows, width = in_hbm.shape
    half = rows // 2
    row, col, c = lax.axis_index("row"), lax.axis_index("col"), lax.axis_index("depth")
    z, h = row // 2, row % 2
    yl, x = col // 4, col % 4

    def along_z(step):
        return (((z + step + 8) % 8) * 2 + h, col, c)

    def along_x(step):
        return (row, yl * 4 + (x + step + 4) % 4, c)

    y_far = (z * 2 + 1 - h, col, c)
    y_near = (row, (1 - yl) * 4 + x, c)
    sibling = (row, col, 1 - c)

    ids = {}
    sent = []

    def remote(key, src, dst, target):
        k = ids.setdefault(key, len(ids))
        assert k < N_SEM
        return pltpu.make_async_remote_copy(
            src_ref=src,
            dst_ref=dst,
            send_sem=send_sem.at[k],
            recv_sem=recv_sem.at[k],
            device_id=target,
            device_id_type=MESH,
        )

    def chunk(ch):
        return pl.ds(ch * half, half)

    def og_at(zrel, s):
        return ((z + zrel + 8) % 8) * 2 + (h if s == 0 else 1 - h)

    def z_copy(way, d, s, ch, receiving):
        zrel = -way * d if receiving else -way * (d - 1)
        dst = og.at[og_at(zrel, s), chunk(ch)]
        src = og_hbm.at[chunk(ch)] if d == 1 and s == 0 and not receiving else dst
        return remote(("z", way, d, s, ch), src, dst, along_z(way))

    def y_copy(zrel, ch, receiving):
        dst = og.at[og_at(zrel, 1 if receiving else 0), chunk(ch)]
        src = og_hbm.at[chunk(ch)] if zrel == 0 and not receiving else dst
        return remote(("y", zrel, ch), src, dst, y_far)

    def col_of(s, xrel):
        return (yl if s == 0 else 1 - yl) * 4 + (x + xrel + 4) % 4

    def x_copy(way, d, s, ch, receiving):
        xrel = -way * d if receiving else -way * (d - 1)
        dst = inp.at[col_of(s, xrel) * 2 + c, chunk(ch)]
        src = in_hbm.at[chunk(ch)] if d == 1 and s == 0 and not receiving else dst
        return remote(("x", way, d, s, ch), src, dst, along_x(way))

    def l_copy(ch, receiving):
        dst = inp.at[col_of(1 if receiving else 0, 0) * 2 + c, chunk(ch)]
        src = dst if receiving else in_hbm.at[chunk(ch)]
        return remote(("l", ch), src, dst, y_near)

    def c_copy(s, xrel, receiving):
        dst = inp.at[col_of(s, xrel) * 2 + (1 - c if receiving else c)]
        src = in_hbm if s == 0 and xrel == 0 and not receiving else dst
        return remote(("c", s, xrel % 4), src, dst, sibling)

    def send(copy_of, *key):
        copy = copy_of(*key, False)
        copy.start()
        sent.append((None, copy))

    def receive(copy_of, *key):
        copy_of(*key, True).wait_recv()

    def mine(s):
        return c == h if s == 0 else c != h

    def slot(b):
        return ZS.index(b[0]) * 2 + b[1]

    def from_root(b):
        return (x - (z + b[0]) + 12) % 4

    def root_y(b):
        return ((z + b[0] + 8) % 8) // 4

    def p_copy(b):
        return remote(("p",) + b, part.at[slot(b)], from_core.at[ZS.index(b[0])], sibling)

    def tree_copy(way, b, ch):
        landing = from_up if way == -1 else from_down
        return remote(
            ("t", way, b[0], ch),
            part.at[slot(b), chunk(ch)],
            landing.at[ZS.index(b[0]), chunk(ch)],
            along_x(way),
        )

    def root_copy(b):
        return remote(("r",), part.at[slot(b)], from_y, y_near)

    def send_when(cond, copies):
        @pl.when(cond)
        def _():
            for copy in copies:
                copy.start()

        sent.append((cond, copies))

    def partial(blocks):
        value = jnp.concatenate([og[og_at(*b)] for b in blocks], 0)
        sums = dot3(split(value), (w_hi[...], w_lo[...]), ((1,), (1,)))
        for i, b in enumerate(blocks):
            part[slot(b)] = sums[i * rows : (i + 1) * rows]
        for b in blocks:
            send_when(jnp.logical_not(mine(b[1])), [p_copy(b)])

    def rs_b(*blocks):
        for b in blocks:
            @pl.when(mine(b[1]))
            def _():
                p_copy(b).wait_recv()
                part[slot(b)] += from_core[ZS.index(b[0])]

            at = from_root(b)
            send_when(mine(b[1]) & (at == 2), [tree_copy(-1, b, 0), tree_copy(1, b, 1)])
            send_when(mine(b[1]) & (at == 1), [tree_copy(-1, b, 1)])
            send_when(mine(b[1]) & (at == 3), [tree_copy(1, b, 0)])

    def rs_c(*blocks):
        for b in blocks:
            at = from_root(b)
            for place, way, ch in ((1, -1, 0), (3, 1, 1)):
                cond = mine(b[1]) & (at == place)
                landing = from_up if way == -1 else from_down

                @pl.when(cond)
                def _():
                    tree_copy(way, b, ch).wait_recv()
                    part[slot(b), ch * half : (ch + 1) * half] += landing[
                        ZS.index(b[0]), ch * half : (ch + 1) * half
                    ]

                send_when(cond, [tree_copy(way, b, ch)])

    def rs_d(*blocks):
        for b in blocks:
            cond = mine(b[1]) & (from_root(b) == 0)

            @pl.when(cond)
            def _():
                for way in (-1, 1):
                    for ch in (0, 1):
                        tree_copy(way, b, ch).wait_recv()
                i = ZS.index(b[0])
                part[slot(b)] += from_up[i] + from_down[i]

            send_when(cond & (root_y(b) != yl), [root_copy(b)])

    def rs_e(*blocks):
        for b in blocks:
            @pl.when(mine(b[1]) & (from_root(b) == 0) & (root_y(b) == yl))
            def _():
                root_copy(b).wait_recv()
                part[slot(b)] += from_y[...]
                copy = pltpu.make_async_copy(part.at[slot(b)], ig_hbm, local_sem.at[3])
                copy.start()
                copy.wait()

    def weight_sum(zrel, first=False):
        block = pl.ds(((z + zrel + 8) % 8) * 2, 2)
        left = inp[block].reshape(2 * rows, width).T
        right = og[block].reshape(2 * rows, width)
        sums = dot3(split(left), split(right), ((1,), (0,)))
        wg[...] = sums if first else wg[...] + sums

    both = (1, -1)

    barrier = pltpu.get_barrier_semaphore()
    neighbours = [along_z(1), along_z(-1), along_x(1), along_x(-1), y_far, y_near, sibling]
    for device in neighbours:
        pl.semaphore_signal(barrier, inc=1, device_id=device, device_id_type=MESH)
    own_w = pltpu.make_async_copy(w_hbm, w, local_sem.at[0])
    own_og = pltpu.make_async_copy(og_hbm, og.at[og_at(0, 0)], local_sem.at[1])
    own_in = pltpu.make_async_copy(in_hbm, inp.at[col * 2 + c], local_sem.at[2])
    for copy in (own_og, own_w, own_in):
        copy.start()
    pl.semaphore_wait(barrier, len(neighbours))

    for ch in (0, 1):
        for way in both:
            send(z_copy, way, 1, 0, ch)
        send(y_copy, 0, ch)
        for way in both:
            send(x_copy, way, 1, 0, ch)
    send(c_copy, 0, 0)
    for ch in (0, 1):
        send(l_copy, ch)
    own_w.wait()
    w_hi[...], w_lo[...] = split(w[...])
    own_og.wait()
    own_in.wait()
    partial([(0, 0)])

    for way in both:
        receive(z_copy, way, 1, 0, 0)
        send(z_copy, way, 2, 0, 0)
        send(y_copy, -way, 0)
    for way in both:
        receive(x_copy, way, 1, 0, 0)
    send(x_copy, 1, 2, 0, 0)
    for way in both:
        receive(z_copy, way, 1, 0, 1)
        send(z_copy, way, 2, 0, 1)
        send(y_copy, -way, 1)
    for way in both:
        receive(x_copy, way, 1, 0, 1)
    send(x_copy, -1, 2, 0, 1)
    for way in both:
        send(c_copy, 0, -way)
    rs_b((0, 0))
    partial([(1, 0), (-1, 0)])
    receive(y_copy, 0, 0)
    receive(y_copy, 0, 1)
    partial([(0, 1)])
    for way in both:
        receive(z_copy, way, 2, 0, 0)
        send(z_copy, way, 3, 0, 0)
    rs_b((1, 0), (-1, 0))
    rs_c((0, 0))
    receive(x_copy, 1, 2, 0, 0)
    receive(x_copy, -1, 2, 0, 1)
    send(c_copy, 0, 2)
    for way in both:
        receive(z_copy, way, 2, 0, 1)
        send(z_copy, way, 3, 0, 1)
    for ch in (0, 1):
        receive(l_copy, ch)
        for way in both:
            send(x_copy, way, 1, 1, ch)
    send(c_copy, 1, 0)
    partial([(2, 0), (-2, 0)])
    rs_b((0, 1))
    rs_c((1, 0), (-1, 0))
    rs_d((0, 0))
    for way in both:
        receive(y_copy, -way, 0)
        send(z_copy, way, 2, 1, 0)
    receive(z_copy, 1, 3, 0, 0)
    send(z_copy, 1, 4, 0, 0)
    receive(z_copy, -1, 3, 0, 0)
    rs_b((2, 0), (-2, 0))
    rs_c((0, 1))
    rs_d((1, 0), (-1, 0))
    receive(z_copy, 1, 3, 0, 1)
    receive(z_copy, -1, 3, 0, 1)
    send(z_copy, -1, 4, 0, 1)
    for way in both:
        receive(y_copy, -way, 1)
        send(z_copy, way, 2, 1, 1)
    partial([(3, 0), (-3, 0)])
    partial([(1, 1), (-1, 1)])
    for ch in (0, 1):
        for way in both:
            receive(x_copy, way, 1, 1, ch)
        way = 1 if ch == 0 else -1
        send(x_copy, way, 2, 1, ch)
    for way in both:
        send(c_copy, 1, -way)
    rs_c((2, 0), (-2, 0))
    rs_d((0, 1))
    receive(z_copy, 1, 4, 0, 0)
    send(y_copy, 4, 0)
    receive(z_copy, -1, 4, 0, 1)
    send(y_copy, 4, 1)
    rs_b((1, 1), (-1, 1), (3, 0), (-3, 0))
    partial([(4, 0)])
    receive(x_copy, 1, 2, 1, 0)
    receive(x_copy, -1, 2, 1, 1)
    send(c_copy, 1, 2)
    rs_d((2, 0), (-2, 0))
    for way in both:
        receive(z_copy, way, 2, 1, 0)
        send(z_copy, way, 3, 1, 0)
    rs_c((1, 1), (-1, 1), (3, 0), (-3, 0))
    rs_b((4, 0))
    for s, xrel in ((0, 0), (0, 1), (0, -1), (0, 2), (1, 0), (1, 1), (1, -1), (1, 2)):
        receive(c_copy, s, xrel)
    weight_sum(0, first=True)
    for way in both:
        receive(z_copy, way, 2, 1, 1)
        send(z_copy, way, 3, 1, 1)
    partial([(2, 1), (-2, 1)])
    rs_d((1, 1), (-1, 1), (3, 0), (-3, 0))
    rs_c((4, 0))
    weight_sum(1)
    rs_b((2, 1), (-2, 1))
    weight_sum(-1)
    receive(y_copy, 4, 0)
    receive(y_copy, 4, 1)
    partial([(4, 1)])
    weight_sum(2)
    rs_c((2, 1), (-2, 1))
    rs_d((4, 0))
    rs_b((4, 1))
    weight_sum(-2)
    weight_sum(4)
    for way in both:
        receive(z_copy, way, 3, 1, 0)
        receive(z_copy, way, 3, 1, 1)
    partial([(3, 1), (-3, 1)])
    rs_c((4, 1))
    rs_d((2, 1), (-2, 1))
    rs_b((3, 1), (-3, 1))
    weight_sum(3)
    rs_c((3, 1), (-3, 1))
    weight_sum(-3)
    out = pltpu.make_async_copy(wg, wg_hbm, local_sem.at[0])
    out.start()
    rs_d((4, 1), (3, 1), (-3, 1))
    rs_e(*((zrel, s) for zrel in ZS for s in (0, 1)))
    out.wait()
    for cond, copies in sent:
        if cond is None:
            copies.wait_send()
        else:
            @pl.when(cond)
            def _():
                for copy in copies:
                    copy.wait_send()


def solution(mesh):
    def local(inputs, out_grad, weight):
        rows, width = inputs.shape
        features = weight.shape[0]
        vmem = pltpu.VMEM
        dma = pltpu.SemaphoreType.DMA
        return pl.pallas_call(
            kernel,
            out_shape=(
                jax.ShapeDtypeStruct((rows, features), F32),
                jax.ShapeDtypeStruct(weight.shape, F32),
            ),
            in_specs=[pl.BlockSpec(memory_space=pl.ANY)] * 3,
            out_specs=[pl.BlockSpec(memory_space=pl.ANY)] * 2,
            scratch_shapes=[
                vmem((16, rows, width), F32),
                vmem((16, rows, width), F32),
                vmem(weight.shape, F32),
                vmem(weight.shape, BF16),
                vmem(weight.shape, BF16),
                vmem((16, rows, features), F32),
                vmem((8, rows, features), F32),
                vmem((8, rows, features), F32),
                vmem((8, rows, features), F32),
                vmem((rows, features), F32),
                vmem(weight.shape, F32),
                dma((4,)),
                dma((N_SEM,)),
                dma((N_SEM,)),
            ],
            compiler_params=pltpu.CompilerParams(
                collective_id=0,
                has_side_effects=True,
                vmem_limit_bytes=56 * 2**20,
            ),
        )(inputs, out_grad, weight)

    placed = (P(("col", "depth"), "row"), P("row", ("col", "depth")), P("row", ("col", "depth")))
    return jax.shard_map(
        local,
        mesh=mesh,
        in_specs=placed,
        out_specs=(P(("col", "depth"), "row"), P("row", ("col", "depth"))),
        check_vma=False,
    )
```

time: 257 us -> 108 us (0.42); the launches traced: 252 us -> 107 us
  waiting for transfers between devices: 199 us -> 0 us
  Pallas kernels: 0 us -> 102 us
  matrix products: 39 us -> 0 us
  between operations: 13.8 us -> 0.64 us
  local copies, waits for them, and re-layouts: 0.01 us -> 4.99 us
    all_gather x2 -> x0, waiting for transfers between devices: 145 us -> none  [the longest x1 118 us: local(): grad_all = lax.all_gather(out_grad, 'row', axis=0, tiled=True)]
    pallas_call x0 -> x1, Pallas kernels: none -> 102 us  [local(): pl.pallas_call(kernel, out_shape=(jax.ShapeDtypeStruct((rows, features),...]
    reduce_scatter x1 -> x0, waiting for transfers between devices: 53.4 us -> none  [local(): lax.psum_scatter(contract_cols(grad_all, weight), ('col', 'depth'), scatt...]
    dot_general x2 -> x0, matrix products: 39 us -> none  [the longest x1 20 us: contract_rows(): lax.dot_general(left, right, (((0,), (0,)), ((), ())), precision=lax.Prec...]
    unnamed x2, local copies, waits for them, and re-layouts: 0.01 us -> 4.99 us
  transfers between devices with their start and end apart: 3 -> 0, of which waited for: 3 -> 0; matrix products, arithmetic and copies ran while one was open for 15% -> 0% of each run, Pallas kernels for 0% -> 0%
where the time goes in v1:
time: 108 us; the launch traced here: 107 us
  Pallas kernels  102 us (94%)
  local copies, waits for them, and re-layouts  4.99 us (5%)
    pallas_call x1, Pallas kernels, local(): pl.pallas_call(kernel, out_shape=(jax.ShapeDtypeStruct((rows, features),...  102 us
    unnamed x2, local copies, waits for them, and re-layouts  4.99 us

profile of v1, /device:TPU:22, one launch (start us, length us, event | category | flops | bytes accessed | tf_op | source)
XLA Modules:
  0.0 107.3 jit_solution(16929952398276096811)
XLA Ops:
  0.6 101.7 %shard_map.50 = (f32[128,768]{1,0:T(8,128)}, f32[768,768]{1,0:T(8,128)}) custom-call(f32[128,768]{1,0:T(8,128)} %in_hbm.1, f32[128,768]{1,0:T(8,128)} %og_hbm.1, f32[768,768]{1,0:T(8,128)} %w_hbm.1), custom_call_target="tpu_custom_call" | custom-call | tf_op jit(solution)/shard_map/pallas_call | solution.py:371
  102.3 1.8 %copy.7 = f32[128,768]{1,0:T(8,128)} copy(f32[128,768]{1,0:T(8,128)} %get-tuple-element.4) | data formatting | bytes 786432
  104.1 3.2 %copy.8 = f32[768,768]{1,0:T(8,128)} copy(f32[768,768]{1,0:T(8,128)} %get-tuple-element.5) | data formatting | bytes 4718592

commit v2 on v0

v2 whole, which is shorter than its diff:
```python
import jax
import jax.numpy as jnp
from jax import lax
from jax.experimental import pallas as pl
from jax.experimental.pallas import tpu as pltpu
from jax.sharding import PartitionSpec as P

MESH = pl.DeviceIdType.MESH
F32 = jnp.float32
BF16 = jnp.bfloat16
N_SEM = 208
NCP = 4
PIECES = ((0, 64), (64, 32), (96, 32))
GROUPS = (
    ((0, 0),),
    ((1, 0), (-1, 0)),
    ((0, 1),),
    ((2, 0), (-2, 0)),
    ((3, 0), (-3, 0)),
    ((4, 0),),
    ((2, 1), (-2, 1)),
    ((1, 1), (-1, 1)),
    ((4, 1),),
    ((3, 1), (-3, 1)),
)
PAIRS = (
    ((0, 0), (1, 0)),
    ((-1, 0), (2, 0)),
    ((-2, 0), (3, 0)),
    ((-3, 0), (4, 0)),
    ((0, 1), (2, 1)),
    ((-2, 1), (1, 1)),
    ((-1, 1), (4, 1)),
    ((3, 1), (-3, 1)),
)
TIMES = {
    "begin": 0,
    "ysend": 1,
    ("p", (0, 0), 0): 2,
    ("z", 1, 1, 0, 0): 3,
    ("z", -1, 1, 0, 0): 4,
    ("x", -1, 1, 0, 0): 5,
    ("x", 1, 1, 0, 0): 6,
    ("l", 0): 7,
    ("x", -1, 1, 0, 1): 8,
    ("z", 1, 1, 0, 64): 9,
    ("z", -1, 1, 0, 64): 10,
    ("x", 1, 1, 0, 1): 11,
    ("p", (1, 0), 0): 12,
    ("b", (0, 0), 0): 13,
    ("b", (1, 0), 0): 14,
    ("b", (-1, 0), 0): 15,
    ("z", 1, 2, 0, 0): 16,
    ("l", 1): 17,
    ("z", -1, 2, 0, 0): 18,
    ("c", (0, 0), 0): 19,
    ("x", -1, 1, 1, 0): 20,
    ("x", 1, 2, 0, 0): 21,
    ("y", 0, 0): 22,
    ("x", 1, 1, 1, 0): 23,
    ("x", -1, 2, 0, 1): 24,
    ("z", 1, 2, 0, 64): 25,
    ("z", -1, 2, 0, 64): 26,
    ("p", (2, 0), 0): 27,
    ("b", (-2, 0), 0): 28,
    ("xl", 0): 29,
    ("y", 0, 1): 30,
    ("p", (0, 1), 0): 31,
    ("b", (2, 0), 0): 32,
    ("z", 1, 3, 0, 0): 33,
    ("b", (0, 1), 0): 34,
    ("y", -2, 0): 35,
    ("x", -1, 1, 1, 1): 36,
    ("z", -1, 3, 0, 64): 37,
    ("c", (1, 0), 0): 38,
    ("c", (-1, 0), 0): 39,
    ("x", 1, 1, 1, 1): 40,
    ("z", 1, 3, 0, 64): 41,
    ("z", -1, 3, 0, 0): 42,
    ("p", (3, 0), 0): 43,
    ("zo", 0): 44,
    ("zo", 1): 45,
    ("c", (2, 0), 0): 46,
    ("y", 2, 0): 47,
    ("b", (3, 0), 0): 48,
    ("d", (0, 0), 0): 49,
    ("b", (-3, 0), 0): 50,
    ("c", (0, 1), 0): 51,
    ("c", (-2, 0), 0): 52,
    ("y", -2, 1): 53,
    ("z", 1, 4, 0, 0): 54,
    ("x", 1, 2, 1, 0): 55,
    ("y", 2, 1): 56,
    ("x", -1, 2, 1, 1): 57,
    ("xl", 1): 58,
    ("p", (2, 1), 0): 59,
    ("z", -1, 4, 0, 64): 60,
    ("d", (2, 0), 0): 61,
    ("p", (4, 0), 0): 62,
    ("z", 1, 3, 1, 0): 63,
    ("d", (-1, 0), 0): 64,
    ("d", (0, 1), 0): 65,
    ("d", (1, 0), 0): 66,
    ("z", -1, 1, 1, 0): 67,
    ("b", (2, 1), 0): 68,
    ("c", (-3, 0), 0): 69,
    ("c", (3, 0), 0): 70,
    ("b", (-2, 1), 0): 71,
    ("z", 1, 1, 1, 0): 72,
    "cwait": 73,
    ("wg", 0): 74,
    ("b", (4, 0), 0): 75,
    ("wg", 1): 76,
    ("d", (-2, 0), 0): 77,
    ("wg", 2): 78,
    ("z", 1, 1, 1, 64): 79,
    ("y", 4, 0): 80,
    ("wg", 3): 81,
    ("z", -1, 1, 1, 64): 82,
    ("p", (1, 1), 0): 83,
    ("wg", 4): 84,
    ("c", (2, 1), 0): 85,
    ("z", -1, 3, 1, 0): 86,
    ("c", (4, 0), 0): 87,
    ("d", (3, 0), 0): 88,
    ("p", (3, 1), 0): 89,
    ("d", (-3, 0), 0): 90,
    ("y", 4, 1): 91,
    ("p", (4, 1), 0): 92,
    ("c", (-2, 1), 0): 93,
    ("b", (1, 1), 0): 94,
    ("z", -1, 3, 1, 64): 95,
    ("z", 1, 3, 1, 96): 96,
    ("b", (-1, 1), 0): 97,
    ("b", (3, 1), 0): 98,
    ("z", -1, 3, 1, 96): 99,
    ("wg", 5): 100,
    ("b", (-3, 1), 0): 101,
    ("z", 1, 3, 1, 64): 102,
    ("p", (3, 1), 96): 103,
    ("b", (4, 1), 0): 104,
    ("b", (3, 1), 96): 105,
    ("d", (2, 1), 0): 106,
    ("wg", 6): 107,
    ("b", (-3, 1), 96): 108,
    ("p", (3, 1), 64): 109,
    ("b", (3, 1), 64): 110,
    ("b", (-3, 1), 64): 111,
    ("c", (-3, 1), 0): 112,
    ("d", (4, 0), 0): 113,
    ("c", (-1, 1), 0): 114,
    ("d", (-2, 1), 0): 115,
    ("c", (1, 1), 0): 116,
    ("wg", 7): 117,
    ("c", (4, 1), 0): 118,
    ("c", (-3, 1), 64): 119,
    ("c", (3, 1), 0): 120,
    ("c", (3, 1), 64): 121,
    ("c", (3, 1), 96): 122,
    ("d", (-1, 1), 0): 123,
    ("c", (-3, 1), 96): 124,
    "out": 125,
    ("d", (3, 1), 0): 126,
    ("d", (-3, 1), 0): 127,
    ("d", (1, 1), 0): 128,
    ("d", (4, 1), 0): 129,
    ("d", (-3, 1), 64): 130,
    ("d", (3, 1), 64): 131,
    ("d", (3, 1), 96): 132,
    ("d", (-3, 1), 96): 133,
    ("e", 0): 134,
    ("e", 64): 135,
    ("e", 96): 136,
    "end": 137,
}


def split(value):
    high = value.astype(BF16)
    return high, (value - high.astype(F32)).astype(BF16)


def dot3(left, right, dims):
    def one(a, b):
        return lax.dot_general(a, b, (dims, ((), ())), preferred_element_type=F32)

    return one(left[0], right[0]) + one(left[0], right[1]) + one(left[1], right[0])


def kernel(
    in_hbm, og_hbm, w_hbm, ig_hbm, wg_hbm,
    og, inp, w, w_hi, w_lo, part, from_core, from_up, from_down, from_y, wg, v_hi, v_lo,
    local_sem, send_sem, recv_sem,
):
    rows, width = in_hbm.shape
    half = rows // 2
    row, col, c = lax.axis_index("row"), lax.axis_index("col"), lax.axis_index("depth")
    z, h = row // 2, row % 2
    yl, x = col // 4, col % 4

    def along_z(step):
        return (((z + step + 8) % 8) * 2 + h, col, c)

    def along_x(step):
        return (row, yl * 4 + (x + step + 4) % 4, c)

    y_far = (z * 2 + 1 - h, col, c)
    y_near = (row, (1 - yl) * 4 + x, c)
    sibling = (row, col, 1 - c)

    ids = {}
    sent = []

    def remote(key, src, dst, target):
        k = ids.setdefault(key, len(ids))
        assert k < N_SEM
        return pltpu.make_async_remote_copy(
            src_ref=src,
            dst_ref=dst,
            send_sem=send_sem.at[k],
            recv_sem=recv_sem.at[k],
            device_id=target,
            device_id_type=MESH,
        )

    def chunk(ch):
        return pl.ds(ch * half, half)

    def og_at(zrel, s):
        return ((z + zrel + 8) % 8) * 2 + (h if s == 0 else 1 - h)

    def z_copy(way, d, s, lo, n, receiving):
        zrel = -way * d if receiving else -way * (d - 1)
        cut = pl.ds(lo, n)
        dst = og.at[og_at(zrel, s), cut]
        src = og_hbm.at[cut] if d == 1 and s == 0 and not receiving else dst
        return remote(("z", way, d, s, lo), src, dst, along_z(way))

    def y_copy(zrel, ch, receiving):
        dst = og.at[og_at(zrel, 1 if receiving else 0), chunk(ch)]
        src = og_hbm.at[chunk(ch)] if zrel == 0 and not receiving else dst
        return remote(("y", zrel, ch), src, dst, y_far)

    def col_of(s, xrel):
        return (yl if s == 0 else 1 - yl) * 4 + (x + xrel + 4) % 4

    def x_copy(way, d, s, ch, receiving):
        xrel = -way * d if receiving else -way * (d - 1)
        dst = inp.at[col_of(s, xrel) * 2 + c, chunk(ch)]
        src = in_hbm.at[chunk(ch)] if d == 1 and s == 0 and not receiving else dst
        return remote(("x", way, d, s, ch), src, dst, along_x(way))

    def l_copy(ch, receiving):
        dst = inp.at[col_of(1 if receiving else 0, 0) * 2 + c, chunk(ch)]
        src = dst if receiving else in_hbm.at[chunk(ch)]
        return remote(("l", ch), src, dst, y_near)

    def c_copy(s, xrel, receiving):
        dst = inp.at[col_of(s, xrel) * 2 + (1 - c if receiving else c)]
        src = in_hbm if s == 0 and xrel == 0 and not receiving else dst
        return remote(("c", s, xrel % 4), src, dst, sibling)

    def send(copy_of, *key):
        copy = copy_of(*key, False)
        copy.start()
        sent.append((None, copy))

    def receive(copy_of, *key):
        copy_of(*key, True).wait_recv()

    def mine(b):
        return c == h if b[1] == 0 else c != h

    def slot(b):
        return b[0] % 8 * 2 + b[1]

    def from_root(b):
        return (x - (z + b[0]) + 12) % 4

    def root_y(b):
        return ((z + b[0] + 8) % 8) // 4

    def p_copy(b, lo, n):
        cut = pl.ds(lo, n)
        return remote(
            ("p", b, lo), part.at[slot(b), cut], from_core.at[b[0] % 8, cut], sibling
        )

    def tree_copy(way, b, lo, n):
        landing = from_up if way == -1 else from_down
        cut = pl.ds(lo, n)
        return remote(
            ("t", way, b[0], lo),
            part.at[slot(b), cut],
            landing.at[b[0] % 8, cut],
            along_x(way),
        )

    def root_copy(b, lo, n):
        cut = pl.ds(lo, n)
        return remote(("r", lo), part.at[slot(b), cut], from_y.at[cut], y_near)

    def send_when(cond, copies):
        @pl.when(cond)
        def _():
            for copy in copies:
                copy.start()

        sent.append((cond, copies))

    def partial(blocks, lo, n):
        m = len(blocks) * n
        value = jnp.concatenate([og[og_at(*b), lo : lo + n] for b in blocks], 0)
        v_hi[:m], v_lo[:m] = split(value)

        @pl.loop(0, width // 256)
        def _(i):
            cut = pl.ds(pl.multiple_of(i * 256, 256), 256)
            sums = dot3((v_hi[:m], v_lo[:m]), (w_hi[cut], w_lo[cut]), ((1,), (1,)))
            for k, b in enumerate(blocks):
                part[slot(b), lo : lo + n, cut] = sums[k * n : (k + 1) * n]

        for b in blocks:
            send_when(jnp.logical_not(mine(b)), [p_copy(b, lo, n)])

    def rs_b(blocks, lo, n):
        hn = n // 2
        for b in blocks:
            @pl.when(mine(b))
            def _():
                p_copy(b, lo, n).wait_recv()
                part[slot(b), lo : lo + n] += from_core[b[0] % 8, lo : lo + n]

            at = from_root(b)
            send_when(mine(b) & (at == 2), [tree_copy(-1, b, lo, hn), tree_copy(1, b, lo + hn, hn)])
            send_when(mine(b) & (at == 1), [tree_copy(-1, b, lo + hn, hn)])
            send_when(mine(b) & (at == 3), [tree_copy(1, b, lo, hn)])

    def rs_c(blocks, lo, n):
        hn = n // 2
        for b in blocks:
            at = from_root(b)
            for place, way, lo_ in ((1, -1, lo), (3, 1, lo + hn)):
                cond = mine(b) & (at == place)
                landing = from_up if way == -1 else from_down

                @pl.when(cond)
                def _():
                    tree_copy(way, b, lo_, hn).wait_recv()
                    part[slot(b), lo_ : lo_ + hn] += landing[b[0] % 8, lo_ : lo_ + hn]

                send_when(cond, [tree_copy(way, b, lo_, hn)])

    def rs_d(blocks, lo, n):
        hn = n // 2
        for b in blocks:
            cond = mine(b) & (from_root(b) == 0)

            @pl.when(cond)
            def _():
                for way in (-1, 1):
                    for lo_ in (lo, lo + hn):
                        tree_copy(way, b, lo_, hn).wait_recv()
                i = b[0] % 8
                part[slot(b), lo : lo + n] += (
                    from_up[i, lo : lo + n] + from_down[i, lo : lo + n]
                )

            send_when(
                cond & (root_y(b) != yl),
                [root_copy(b, *p) for p in PIECES if lo <= p[0] < lo + n],
            )

    own_slot = (col - z + 8) % 8 * 2 + (c + h) % 2

    def own_out(lo, n):
        cut = pl.ds(lo, n)
        return pltpu.make_async_copy(
            part.at[own_slot, cut], ig_hbm.at[cut], local_sem.at[3 + PIECES.index((lo, n))]
        )

    def rs_e(lo, n):
        root_copy((0, 0), lo, n).wait_recv()
        part[own_slot, lo : lo + n] += from_y[lo : lo + n]
        own_out(lo, n).start()

    def weight_sum(blocks, first):
        places = [og_at(*b) for b in blocks]
        v_hi[...], v_lo[...] = split(jnp.concatenate([og[t] for t in places], 0))

        @pl.loop(0, width // 256)
        def _(i):
            cut = pl.ds(pl.multiple_of(i * 256, 256), 256)
            left = jnp.concatenate([inp[t, :, cut] for t in places], 0).T
            sums = dot3(split(left), (v_hi[...], v_lo[...]), ((1,), (0,)))
            wg[cut] = sums if first else wg[cut] + sums

    both = (1, -1)

    barrier = pltpu.get_barrier_semaphore()
    neighbours = [along_z(1), along_z(-1), along_x(1), along_x(-1), y_far, y_near, sibling]
    for device in neighbours:
        pl.semaphore_signal(barrier, inc=1, device_id=device, device_id_type=MESH)
    own_w = pltpu.make_async_copy(w_hbm, w, local_sem.at[0])
    own_og = pltpu.make_async_copy(og_hbm, og.at[og_at(0, 0)], local_sem.at[1])
    own_in = pltpu.make_async_copy(in_hbm, inp.at[col * 2 + c], local_sem.at[2])
    for copy in (own_og, own_w, own_in):
        copy.start()
    pl.semaphore_wait(barrier, len(neighbours))

    steps = []

    def at(key, step, *args):
        steps.append((TIMES[key], len(steps), key, step, args))

    def begin():
        for ch in (0, 1):
            for way in both:
                send(z_copy, way, 1, 0, ch * half, half)
            for way in both:
                send(x_copy, way, 1, 0, ch)
            send(l_copy, ch)
        send(c_copy, 0, 0)
        own_og.wait()
        own_w.wait()
        w_hi[...], w_lo[...] = split(w[...])
        own_in.wait()

    def y_send():
        for ch in (0, 1):
            send(y_copy, 0, ch)

    def z_step(way, d, s, lo, n):
        receive(z_copy, way, d, s, lo, n)
        if s == 0 and (d < 3 or d == 3 and way == (1 if lo == 0 else -1)):
            send(z_copy, way, d + 1, 0, lo, n)
        if s == 0 and d == 2:
            send(y_copy, -2 * way, lo // half)
        if s == 0 and d == 4:
            send(y_copy, 4, lo // half)

    def y_step(zrel, ch):
        receive(y_copy, zrel, ch)
        if abs(zrel) == 2:
            for lo, n in PIECES:
                if lo // half == ch:
                    send(z_copy, -zrel // 2, 3, 1, lo, n)

    def z_other(ch):
        for way in both:
            send(z_copy, way, 1, 1, ch * half, half)

    def x_step(way, d, s, ch):
        receive(x_copy, way, d, s, ch)
        if d == 1 and way == (1, -1)[ch]:
            send(x_copy, way, 2, s, ch)
        if d == 1 and ch == 1:
            send(c_copy, s, -way)

    def x_last(s):
        send(c_copy, s, 2)

    def l_step(ch):
        receive(l_copy, ch)
        for way in both:
            send(x_copy, way, 1, 1, ch)
        if ch == 1:
            send(c_copy, 1, 0)

    def c_wait():
        for s in (0, 1):
            for xrel in (0, 1, -1, 2):
                receive(c_copy, s, xrel)

    at("begin", begin)
    at("ysend", y_send)
    for ch in (0, 1):
        lo = ch * half
        for way in both:
            for d in (1, 2, 3):
                at(("z", way, d, 0, lo), z_step, way, d, 0, lo, half)
            at(("z", way, 1, 1, lo), z_step, way, 1, 1, lo, half)
            for s in (0, 1):
                at(("x", way, 1, s, ch), x_step, way, 1, s, ch)
        way = both[ch]
        at(("z", way, 4, 0, lo), z_step, way, 4, 0, lo, half)
        for s in (0, 1):
            at(("x", way, 2, s, ch), x_step, way, 2, s, ch)
        at(("zo", ch), z_other, ch)
        for zrel in (0, 2, -2, 4):
            at(("y", zrel, ch), y_step, zrel, ch)
        at(("l", ch), l_step, ch)
    for lo, n in PIECES:
        for way in both:
            at(("z", way, 3, 1, lo), z_step, way, 3, 1, lo, n)
        at(("e", lo), rs_e, lo, n)
    at(("xl", 0), x_last, 0)
    at(("xl", 1), x_last, 1)
    at("cwait", c_wait)
    for blocks in GROUPS:
        for lo, n in PIECES if blocks[0] == (3, 1) else [(0, rows)]:
            at(("p", blocks[0], lo), partial, blocks, lo, n)
            for b in blocks:
                at(("b", b, lo), rs_b, [b], lo, n)
                at(("c", b, lo), rs_c, [b], lo, n)
                at(("d", b, lo), rs_d, [b], lo, n)
    for i, blocks in enumerate(PAIRS):
        at(("wg", i), weight_sum, blocks, i == 0)
    out = pltpu.make_async_copy(wg, wg_hbm, local_sem.at[0])
    at("out", out.start)
    at("end", out.wait)
    for _, _, key, step, args in sorted(steps, key=lambda e: e[:2]):
        step(*args)
    for lo, n in PIECES:
        own_out(lo, n).wait()
    for cond, copies in sent:
        if cond is None:
            copies.wait_send()
        else:
            @pl.when(cond)
            def _():
                for copy in copies:
                    copy.wait_send()


def move(ig_in, wg_in, ig_out, wg_out, ig, wg, sem):
    n = wg_in.shape[0] // NCP
    cuts = [pl.ds(i * n, n) for i in range(NCP)]
    steps = [(wg_in.at[c], wg.at[c], wg_out.at[c]) for c in cuts] + [(ig_in, ig, ig_out)]
    loads = [pltpu.make_async_copy(a, b, sem.at[0, i]) for i, (a, b, _) in enumerate(steps)]
    stores = [pltpu.make_async_copy(b, c, sem.at[1, i]) for i, (_, b, c) in enumerate(steps)]
    for copy in loads:
        copy.start()
    for load, store in zip(loads, stores, strict=True):
        load.wait()
        store.start()
    for store in stores:
        store.wait()


def solution(mesh):
    def local(inputs, out_grad, weight):
        rows, width = inputs.shape
        features = weight.shape[0]
        vmem = pltpu.VMEM
        dma = pltpu.SemaphoreType.DMA
        sums_shape = (
            jax.ShapeDtypeStruct((rows, features), F32),
            jax.ShapeDtypeStruct(weight.shape, F32),
        )
        sums = pl.pallas_call(
            kernel,
            out_shape=sums_shape,
            in_specs=[pl.BlockSpec(memory_space=pl.ANY)] * 3,
            out_specs=[pl.BlockSpec(memory_space=pl.ANY)] * 2,
            scratch_shapes=[
                vmem((16, rows, width), F32),
                vmem((16, rows, width), F32),
                vmem(weight.shape, F32),
                vmem(weight.shape, BF16),
                vmem(weight.shape, BF16),
                vmem((16, rows, features), F32),
                vmem((8, rows, features), F32),
                vmem((8, rows, features), F32),
                vmem((8, rows, features), F32),
                vmem((rows, features), F32),
                vmem(weight.shape, F32),
                vmem((2 * rows, width), BF16),
                vmem((2 * rows, width), BF16),
                dma((8,)),
                dma((N_SEM,)),
                dma((N_SEM,)),
            ],
            compiler_params=pltpu.CompilerParams(
                collective_id=0,
                has_side_effects=True,
                vmem_limit_bytes=56 * 2**20,
            ),
        )(inputs, out_grad, weight)
        return pl.pallas_call(
            move,
            out_shape=sums_shape,
            in_specs=[pl.BlockSpec(memory_space=pl.ANY)] * 2,
            out_specs=[pl.BlockSpec(memory_space=pl.ANY)] * 2,
            scratch_shapes=[vmem((rows, features), F32), vmem(weight.shape, F32), dma((2, NCP + 1))],
        )(*sums)

    placed = (P(("col", "depth"), "row"), P("row", ("col", "depth")), P("row", ("col", "depth")))
    return jax.shard_map(
        local,
        mesh=mesh,
        in_specs=placed,
        out_specs=(P(("col", "depth"), "row"), P("row", ("col", "depth"))),
        check_vma=False,
    )
```

time: 257 us -> 92.3 us (0.36); the launches traced: 252 us -> 91.5 us
  waiting for transfers between devices: 199 us -> 0 us
  Pallas kernels: 0 us -> 90.7 us
  matrix products: 39 us -> 0 us
  between operations: 13.8 us -> 0.8 us
    all_gather x2 -> x0, waiting for transfers between devices: 145 us -> none  [the longest x1 118 us: local(): grad_all = lax.all_gather(out_grad, 'row', axis=0, tiled=True)]
    pallas_call x0 -> x2, Pallas kernels: none -> 90.7 us  [the longest x1 88 us: local(): pl.pallas_call(kernel, out_shape=sums_shape, in_specs=[pl.BlockSpec(memor...]
    reduce_scatter x1 -> x0, waiting for transfers between devices: 53.4 us -> none  [local(): lax.psum_scatter(contract_cols(grad_all, weight), ('col', 'depth'), scatt...]
    dot_general x2 -> x0, matrix products: 39 us -> none  [the longest x1 20 us: contract_rows(): lax.dot_general(left, right, (((0,), (0,)), ((), ())), precision=lax.Prec...]
  transfers between devices with their start and end apart: 3 -> 0, of which waited for: 3 -> 0; matrix products, arithmetic and copies ran while one was open for 15% -> 0% of each run, Pallas kernels for 0% -> 0%
where the time goes in v2:
time: 92.3 us; the launch traced here: 91.5 us
  Pallas kernels  90.7 us (98%)
    pallas_call x1, Pallas kernels, local(): pl.pallas_call(kernel, out_shape=sums_shape, in_specs=[pl.BlockSpec(memor...  88 us
    pallas_call x1, Pallas kernels, local(): pl.pallas_call(move, out_shape=sums_shape, in_specs=[pl.BlockSpec(memory_...  2.67 us

profile of v2, /device:TPU:22, one launch (start us, length us, event | category | flops | bytes accessed | tf_op | source)
XLA Modules:
  0.0 91.5 jit_solution(14556164002817623325)
XLA Ops:
  0.6 88.0 %shard_map.50 = (f32[128,768]{1,0:T(8,128)}, f32[768,768]{1,0:T(8,128)}) custom-call(f32[128,768]{1,0:T(8,128)} %in_hbm.1, f32[128,768]{1,0:T(8,128)} %og_hbm.1, f32[768,768]{1,0:T(8,128)} %w_hbm.1), custom_call_target="tpu_custom_call" | custom-call | tf_op jit(solution)/shard_map/pallas_call | solution.py:551
  88.6 2.7 %shard_map.51 = (f32[128,768]{1,0:T(8,128)}, f32[768,768]{1,0:T(8,128)}) custom-call(f32[128,768]{1,0:T(8,128)} %get-tuple-element.4.ig_in, f32[768,768]{1,0:T(8,128)} %get-tuple-element.5.wg_in), custom_call_target="tpu_custom_call" | custom-call | tf_op jit(solution)/shard_map/pallas_call | solution.py:580

commit v3 on v2

--- a/solution.py
+++ b/solution.py
@@ -8,26 +8,24 @@
 MESH = pl.DeviceIdType.MESH
 F32 = jnp.float32
 BF16 = jnp.bfloat16
-N_SEM = 208
+N_SEM = 240
 NCP = 4
 PIECES = ((0, 64), (64, 32), (96, 32))
+HALVES = ((0, 64), (64, 64))
+WHOLE = ((0, 128),)
 GROUPS = (
-    ((0, 0),),
-    ((1, 0), (-1, 0)),
-    ((0, 1),),
-    ((2, 0), (-2, 0)),
-    ((3, 0), (-3, 0)),
-    ((4, 0),),
-    ((2, 1), (-2, 1)),
-    ((1, 1), (-1, 1)),
-    ((4, 1),),
-    ((3, 1), (-3, 1)),
+    (((0, 0),), WHOLE),
+    (((1, 0), (-1, 0)), WHOLE),
+    (((0, 1),), WHOLE),
+    (((2, 0), (-2, 0)), WHOLE),
+    (((3, 0), (-3, 0)), WHOLE),
+    (((4, 0),), WHOLE),
+    (((2, 1), (-2, 1)), WHOLE),
+    (((1, 1), (-1, 1)), HALVES),
+    (((4, 1),), HALVES),
+    (((3, 1), (-3, 1)), PIECES),
 )
 PAIRS = (
-    ((0, 0), (1, 0)),
-    ((-1, 0), (2, 0)),
-    ((-2, 0), (3, 0)),
-    ((-3, 0), (4, 0)),
     ((0, 1), (2, 1)),
     ((-2, 1), (1, 1)),
     ((-1, 1), (4, 1)),
@@ -37,141 +35,153 @@
     "begin": 0,
     "ysend": 1,
     ("p", (0, 0), 0): 2,
-    ("z", 1, 1, 0, 0): 3,
-    ("z", -1, 1, 0, 0): 4,
-    ("x", -1, 1, 0, 0): 5,
-    ("x", 1, 1, 0, 0): 6,
+    ("b", (0, 0), 0): 3,
+    ("x", 1, 1, 0, 0): 4,
+    ("z", 1, 1, 0, 0): 5,
+    ("x", -1, 1, 0, 0): 6,
     ("l", 0): 7,
-    ("x", -1, 1, 0, 1): 8,
+    ("z", -1, 1, 0, 0): 8,
     ("z", 1, 1, 0, 64): 9,
-    ("z", -1, 1, 0, 64): 10,
-    ("x", 1, 1, 0, 1): 11,
-    ("p", (1, 0), 0): 12,
-    ("b", (0, 0), 0): 13,
-    ("b", (1, 0), 0): 14,
-    ("b", (-1, 0), 0): 15,
+    ("x", 1, 1, 0, 1): 10,
+    ("x", -1, 1, 0, 1): 11,
+    ("l", 1): 12,
+    ("z", -1, 1, 0, 64): 13,
+    ("p", (1, 0), 0): 14,
+    ("z", -1, 2, 0, 0): 15,
     ("z", 1, 2, 0, 0): 16,
-    ("l", 1): 17,
-    ("z", -1, 2, 0, 0): 18,
-    ("c", (0, 0), 0): 19,
-    ("x", -1, 1, 1, 0): 20,
+    ("b", (1, 0), 0): 17,
+    ("c", (0, 0), 0): 18,
+    ("b", (-1, 0), 0): 19,
+    ("y", 0, 0): 20,
     ("x", 1, 2, 0, 0): 21,
-    ("y", 0, 0): 22,
-    ("x", 1, 1, 1, 0): 23,
-    ("x", -1, 2, 0, 1): 24,
-    ("z", 1, 2, 0, 64): 25,
-    ("z", -1, 2, 0, 64): 26,
-    ("p", (2, 0), 0): 27,
-    ("b", (-2, 0), 0): 28,
+    ("x", -1, 1, 1, 0): 22,
+    ("z", 1, 2, 0, 64): 23,
+    ("z", -1, 2, 0, 64): 24,
+    ("p", (2, 0), 0): 25,
+    ("b", (2, 0), 0): 26,
+    ("x", 1, 1, 1, 0): 27,
+    ("x", -1, 2, 0, 1): 28,
     ("xl", 0): 29,
     ("y", 0, 1): 30,
     ("p", (0, 1), 0): 31,
-    ("b", (2, 0), 0): 32,
-    ("z", 1, 3, 0, 0): 33,
+    ("z", 1, 3, 0, 0): 32,
+    ("x", -1, 1, 1, 1): 33,
     ("b", (0, 1), 0): 34,
-    ("y", -2, 0): 35,
-    ("x", -1, 1, 1, 1): 36,
-    ("z", -1, 3, 0, 64): 37,
-    ("c", (1, 0), 0): 38,
-    ("c", (-1, 0), 0): 39,
-    ("x", 1, 1, 1, 1): 40,
+    ("zo", 0): 35,
+    ("y", -2, 0): 36,
+    ("z", -1, 3, 0, 0): 37,
+    ("b", (-2, 0), 0): 38,
+    ("x", 1, 1, 1, 1): 39,
+    ("cw", 0): 40,
     ("z", 1, 3, 0, 64): 41,
-    ("z", -1, 3, 0, 0): 42,
+    ("z", -1, 3, 0, 64): 42,
     ("p", (3, 0), 0): 43,
-    ("zo", 0): 44,
+    ("y", 2, 0): 44,
     ("zo", 1): 45,
     ("c", (2, 0), 0): 46,
-    ("y", 2, 0): 47,
-    ("b", (3, 0), 0): 48,
-    ("d", (0, 0), 0): 49,
-    ("b", (-3, 0), 0): 50,
-    ("c", (0, 1), 0): 51,
+    ("z", 1, 4, 0, 0): 47,
+    ("c", (0, 1), 0): 48,
+    ("b", (3, 0), 0): 49,
+    ("z", -1, 1, 1, 0): 50,
+    ("c", (1, 0), 0): 51,
     ("c", (-2, 0), 0): 52,
-    ("y", -2, 1): 53,
-    ("z", 1, 4, 0, 0): 54,
-    ("x", 1, 2, 1, 0): 55,
-    ("y", 2, 1): 56,
-    ("x", -1, 2, 1, 1): 57,
-    ("xl", 1): 58,
-    ("p", (2, 1), 0): 59,
-    ("z", -1, 4, 0, 64): 60,
-    ("d", (2, 0), 0): 61,
-    ("p", (4, 0), 0): 62,
-    ("z", 1, 3, 1, 0): 63,
-    ("d", (-1, 0), 0): 64,
-    ("d", (0, 1), 0): 65,
-    ("d", (1, 0), 0): 66,
-    ("z", -1, 1, 1, 0): 67,
-    ("b", (2, 1), 0): 68,
-    ("c", (-3, 0), 0): 69,
-    ("c", (3, 0), 0): 70,
-    ("b", (-2, 1), 0): 71,
-    ("z", 1, 1, 1, 0): 72,
-    "cwait": 73,
-    ("wg", 0): 74,
-    ("b", (4, 0), 0): 75,
-    ("wg", 1): 76,
-    ("d", (-2, 0), 0): 77,
-    ("wg", 2): 78,
-    ("z", 1, 1, 1, 64): 79,
-    ("y", 4, 0): 80,
-    ("wg", 3): 81,
-    ("z", -1, 1, 1, 64): 82,
-    ("p", (1, 1), 0): 83,
-    ("wg", 4): 84,
-    ("c", (2, 1), 0): 85,
-    ("z", -1, 3, 1, 0): 86,
-    ("c", (4, 0), 0): 87,
-    ("d", (3, 0), 0): 88,
-    ("p", (3, 1), 0): 89,
-    ("d", (-3, 0), 0): 90,
-    ("y", 4, 1): 91,
-    ("p", (4, 1), 0): 92,
-    ("c", (-2, 1), 0): 93,
-    ("b", (1, 1), 0): 94,
-    ("z", -1, 3, 1, 64): 95,
-    ("z", 1, 3, 1, 96): 96,
-    ("b", (-1, 1), 0): 97,
-    ("b", (3, 1), 0): 98,
-    ("z", -1, 3, 1, 96): 99,
-    ("wg", 5): 100,
-    ("b", (-3, 1), 0): 101,
-    ("z", 1, 3, 1, 64): 102,
-    ("p", (3, 1), 96): 103,
-    ("b", (4, 1), 0): 104,
-    ("b", (3, 1), 96): 105,
-    ("d", (2, 1), 0): 106,
-    ("wg", 6): 107,
-    ("b", (-3, 1), 96): 108,
-    ("p", (3, 1), 64): 109,
-    ("b", (3, 1), 64): 110,
-    ("b", (-3, 1), 64): 111,
-    ("c", (-3, 1), 0): 112,
-    ("d", (4, 0), 0): 113,
-    ("c", (-1, 1), 0): 114,
-    ("d", (-2, 1), 0): 115,
-    ("c", (1, 1), 0): 116,
-    ("wg", 7): 117,
-    ("c", (4, 1), 0): 118,
-    ("c", (-3, 1), 64): 119,
-    ("c", (3, 1), 0): 120,
-    ("c", (3, 1), 64): 121,
-    ("c", (3, 1), 96): 122,
-    ("d", (-1, 1), 0): 123,
-    ("c", (-3, 1), 96): 124,
-    "out": 125,
-    ("d", (3, 1), 0): 126,
+    ("b", (-3, 0), 0): 53,
+    ("y", -2, 1): 54,
+    ("c", (-1, 0), 0): 55,
+    ("d", (0, 0), 0): 56,
+    ("x", 1, 2, 1, 0): 57,
+    ("x", -1, 2, 1, 1): 58,
+    ("xl", 1): 59,
+    ("z", 1, 1, 1, 0): 60,
+    ("cw", 1): 61,
+    ("z", -1, 4, 0, 64): 62,
+    ("p", (4, 0), 0): 63,
+    ("d", (2, 0), 0): 64,
+    ("y", 2, 1): 65,
+    ("p", (2, 1), 0): 66,
+    ("p", (1, 1), 0): 67,
+    ("d", (-1, 0), 0): 68,
+    ("b", (2, 1), 0): 69,
+    ("b", (4, 0), 0): 70,
+    ("wg", 0): 71,
+    ("b", (1, 1), 0): 72,
+    ("d", (0, 1), 0): 73,
+    ("c", (-3, 0), 0): 74,
+    ("d", (1, 0), 0): 75,
+    ("c", (3, 0), 0): 76,
+    ("z", 1, 3, 1, 0): 77,
+    ("z", -1, 3, 1, 0): 78,
+    ("y", 4, 0): 79,
+    ("p", (3, 1), 0): 80,
+    ("d", (-2, 0), 0): 81,
+    ("b", (-2, 1), 0): 82,
+    ("b", (-1, 1), 0): 83,
+    ("p", (4, 1), 0): 84,
+    ("wg", 2): 85,
+    ("c", (1, 1), 0): 86,
+    ("b", (3, 1), 0): 87,
+    ("b", (4, 1), 0): 88,
+    ("wg", 1): 89,
+    ("z", -1, 1, 1, 64): 90,
+    ("b", (-3, 1), 0): 91,
+    ("z", 1, 1, 1, 64): 92,
+    ("p", (1, 1), 64): 93,
+    ("wg", 3): 94,
+    ("c", (4, 0), 0): 95,
+    ("z", -1, 3, 1, 64): 96,
+    ("z", 1, 3, 1, 64): 97,
+    ("b", (1, 1), 64): 98,
+    ("y", 4, 1): 99,
+    ("p", (4, 1), 64): 100,
+    ("d", (-3, 0), 0): 101,
+    ("p", (3, 1), 64): 102,
+    ("c", (-1, 1), 0): 103,
+    ("b", (4, 1), 64): 104,
+    ("c", (-3, 1), 0): 105,
+    ("b", (-1, 1), 64): 106,
+    ("c", (3, 1), 0): 107,
+    ("d", (3, 0), 0): 108,
+    ("z", 1, 3, 1, 96): 109,
+    ("z", -1, 3, 1, 96): 110,
+    ("wg", 4): 111,
+    ("c", (2, 1), 0): 112,
+    ("b", (3, 1), 64): 113,
+    ("p", (3, 1), 96): 114,
+    ("b", (-3, 1), 64): 115,
+    ("c", (4, 1), 0): 116,
+    ("wg", 5): 117,
+    ("d", (1, 1), 0): 118,
+    ("b", (3, 1), 96): 119,
+    ("b", (-3, 1), 96): 120,
+    ("c", (-2, 1), 0): 121,
+    ("d", (2, 1), 0): 122,
+    ("c", (1, 1), 64): 123,
+    ("c", (-1, 1), 64): 124,
+    ("d", (-1, 1), 0): 125,
+    ("d", (4, 0), 0): 126,
     ("d", (-3, 1), 0): 127,
-    ("d", (1, 1), 0): 128,
-    ("d", (4, 1), 0): 129,
-    ("d", (-3, 1), 64): 130,
-    ("d", (3, 1), 64): 131,
-    ("d", (3, 1), 96): 132,
-    ("d", (-3, 1), 96): 133,
-    ("e", 0): 134,
-    ("e", 64): 135,
-    ("e", 96): 136,
-    "end": 137,
+    ("c", (4, 1), 64): 128,
+    ("wg", 7): 129,
+    ("c", (3, 1), 64): 130,
+    ("d", (3, 1), 0): 131,
+    ("d", (4, 1), 0): 132,
+    ("c", (-3, 1), 64): 133,
+    ("c", (-3, 1), 96): 134,
+    ("c", (3, 1), 96): 135,
+    ("d", (1, 1), 64): 136,
+    ("d", (-1, 1), 64): 137,
+    ("d", (-2, 1), 0): 138,
+    ("d", (-3, 1), 64): 139,
+    ("wg", 6): 140,
+    ("d", (4, 1), 64): 141,
+    ("d", (3, 1), 64): 142,
+    ("d", (3, 1), 96): 143,
+    ("d", (-3, 1), 96): 144,
+    ("e", 0): 145,
+    "out": 146,
+    ("e", 64): 147,
+    ("e", 96): 148,
+    "end": 149,
 }
 
 
@@ -384,8 +394,7 @@
         part[own_slot, lo : lo + n] += from_y[lo : lo + n]
         own_out(lo, n).start()
 
-    def weight_sum(blocks, first):
-        places = [og_at(*b) for b in blocks]
+    def weight_sum(places, first):
         v_hi[...], v_lo[...] = split(jnp.concatenate([og[t] for t in places], 0))
 
         @pl.loop(0, width // 256)
@@ -467,10 +476,9 @@
         if ch == 1:
             send(c_copy, 1, 0)
 
-    def c_wait():
-        for s in (0, 1):
-            for xrel in (0, 1, -1, 2):
-                receive(c_copy, s, xrel)
+    def c_wait(s):
+        for xrel in (0, 1, -1, 2):
+            receive(c_copy, s, xrel)
 
     at("begin", begin)
     at("ysend", y_send)
@@ -496,16 +504,20 @@
         at(("e", lo), rs_e, lo, n)
     at(("xl", 0), x_last, 0)
     at(("xl", 1), x_last, 1)
-    at("cwait", c_wait)
-    for blocks in GROUPS:
-        for lo, n in PIECES if blocks[0] == (3, 1) else [(0, rows)]:
+    for s in (0, 1):
+        at(("cw", s), c_wait, s)
+    for blocks, pieces in GROUPS:
+        for lo, n in pieces:
             at(("p", blocks[0], lo), partial, blocks, lo, n)
             for b in blocks:
                 at(("b", b, lo), rs_b, [b], lo, n)
                 at(("c", b, lo), rs_c, [b], lo, n)
                 at(("d", b, lo), rs_d, [b], lo, n)
+    for i in range(4):
+        places = [col_of(i // 2, i % 2 * 2 + k) * 2 + h for k in (0, 1)]
+        at(("wg", i), weight_sum, places, i == 0)
     for i, blocks in enumerate(PAIRS):
-        at(("wg", i), weight_sum, blocks, i == 0)
+        at(("wg", 4 + i), weight_sum, [og_at(*b) for b in blocks], False)
     out = pltpu.make_async_copy(wg, wg_hbm, local_sem.at[0])
     at("out", out.start)
     at("end", out.wait)

time: 92.3 us -> 90.1 us (0.976)
  Pallas kernels: 90.7 us -> 88.4 us
    pallas_call x1, Pallas kernels: 88 us -> 85.7 us  [local(): pl.pallas_call(kernel, out_shape=sums_shape, in_specs=[pl.BlockSpec(memor...]
where the time goes in v3:
time: 90.1 us; the launch traced here: 89.2 us
  Pallas kernels  88.4 us (98%)
    pallas_call x1, Pallas kernels, local(): pl.pallas_call(kernel, out_shape=sums_shape, in_specs=[pl.BlockSpec(memor...  85.7 us
    pallas_call x1, Pallas kernels, local(): pl.pallas_call(move, out_shape=sums_shape, in_specs=[pl.BlockSpec(memory_...  2.67 us

profile of v3, /device:TPU:22, one launch (start us, length us, event | category | flops | bytes accessed | tf_op | source)
XLA Modules:
  0.0 89.2 jit_solution(13961765525979879626)
XLA Ops:
  0.6 85.7 %shard_map.50 = (f32[128,768]{1,0:T(8,128)}, f32[768,768]{1,0:T(8,128)}) custom-call(f32[128,768]{1,0:T(8,128)} %in_hbm.1, f32[128,768]{1,0:T(8,128)} %og_hbm.1, f32[768,768]{1,0:T(8,128)} %w_hbm.1), custom_call_target="tpu_custom_call" | custom-call | tf_op jit(solution)/shard_map/pallas_call | solution.py:563
  86.4 2.7 %shard_map.51 = (f32[128,768]{1,0:T(8,128)}, f32[768,768]{1,0:T(8,128)}) custom-call(f32[128,768]{1,0:T(8,128)} %get-tuple-element.4.ig_in, f32[768,768]{1,0:T(8,128)} %get-tuple-element.5.wg_in), custom_call_target="tpu_custom_call" | custom-call | tf_op jit(solution)/shard_map/pallas_call | solution.py:592

commit v4 on v3

--- a/solution.py
+++ b/solution.py
@@ -13,18 +13,24 @@
 PIECES = ((0, 64), (64, 32), (96, 32))
 HALVES = ((0, 64), (64, 64))
 WHOLE = ((0, 128),)
-GROUPS = (
-    (((0, 0),), WHOLE),
-    (((1, 0), (-1, 0)), WHOLE),
-    (((0, 1),), WHOLE),
-    (((2, 0), (-2, 0)), WHOLE),
-    (((3, 0), (-3, 0)), WHOLE),
-    (((4, 0),), WHOLE),
-    (((2, 1), (-2, 1)), WHOLE),
-    (((1, 1), (-1, 1)), HALVES),
-    (((4, 1),), HALVES),
-    (((3, 1), (-3, 1)), PIECES),
-)
+ORDER = (0, 1, -1, 2, -2, 3, -3, 4)
+
+
+def pieces_of(b):
+    return PIECES if b in ((3, 1), (-3, 1)) else HALVES if b in ((1, 1), (-1, 1), (4, 1)) else WHOLE
+
+
+def partial_steps():
+    for b in [(zrel, s) for zrel in ORDER for s in (0, 1)]:
+        if b[1] == 1 and b[0] in (1, 3):
+            for lo in (0, 64):
+                pair = (b, (-b[0], 1))
+                sends = [(q,) + p for q in pair for p in pieces_of(b) if p[0] // 64 == lo // 64]
+                yield ("p", b, lo), [(q, lo) for q in pair], sends
+        elif not (b[1] == 1 and b[0] in (-1, -3)):
+            yield ("p", b, 0), [(b, 0), (b, 64)], [(b,) + p for p in pieces_of(b)]
+
+
 PAIRS = (
     ((0, 1), (2, 1)),
     ((-2, 1), (1, 1)),
@@ -35,153 +41,155 @@
     "begin": 0,
     "ysend": 1,
     ("p", (0, 0), 0): 2,
-    ("b", (0, 0), 0): 3,
-    ("x", 1, 1, 0, 0): 4,
-    ("z", 1, 1, 0, 0): 5,
-    ("x", -1, 1, 0, 0): 6,
-    ("l", 0): 7,
-    ("z", -1, 1, 0, 0): 8,
-    ("z", 1, 1, 0, 64): 9,
+    ("z", 1, 1, 0, 0): 3,
+    ("b", (0, 0), 0): 4,
+    ("z", -1, 1, 0, 0): 5,
+    ("x", 1, 1, 0, 0): 6,
+    ("x", -1, 1, 0, 0): 7,
+    ("l", 0): 8,
+    ("z", -1, 1, 0, 64): 9,
     ("x", 1, 1, 0, 1): 10,
     ("x", -1, 1, 0, 1): 11,
     ("l", 1): 12,
-    ("z", -1, 1, 0, 64): 13,
-    ("p", (1, 0), 0): 14,
-    ("z", -1, 2, 0, 0): 15,
-    ("z", 1, 2, 0, 0): 16,
-    ("b", (1, 0), 0): 17,
+    ("p", (1, 0), 0): 13,
+    ("z", 1, 1, 0, 64): 14,
+    ("p", (-1, 0), 0): 15,
+    ("b", (1, 0), 0): 16,
+    ("z", 1, 2, 0, 0): 17,
     ("c", (0, 0), 0): 18,
     ("b", (-1, 0), 0): 19,
-    ("y", 0, 0): 20,
-    ("x", 1, 2, 0, 0): 21,
-    ("x", -1, 1, 1, 0): 22,
-    ("z", 1, 2, 0, 64): 23,
-    ("z", -1, 2, 0, 64): 24,
-    ("p", (2, 0), 0): 25,
-    ("b", (2, 0), 0): 26,
-    ("x", 1, 1, 1, 0): 27,
-    ("x", -1, 2, 0, 1): 28,
-    ("xl", 0): 29,
-    ("y", 0, 1): 30,
-    ("p", (0, 1), 0): 31,
-    ("z", 1, 3, 0, 0): 32,
-    ("x", -1, 1, 1, 1): 33,
-    ("b", (0, 1), 0): 34,
-    ("zo", 0): 35,
-    ("y", -2, 0): 36,
-    ("z", -1, 3, 0, 0): 37,
-    ("b", (-2, 0), 0): 38,
+    ("z", -1, 2, 0, 0): 20,
+    ("y", 0, 0): 21,
+    ("x", 1, 2, 0, 0): 22,
+    ("x", -1, 1, 1, 0): 23,
+    ("z", 1, 2, 0, 64): 24,
+    ("p", (-2, 0), 0): 25,
+    ("z", -1, 2, 0, 64): 26,
+    ("p", (2, 0), 0): 27,
+    ("b", (2, 0), 0): 28,
+    ("y", 0, 1): 29,
+    ("p", (0, 1), 0): 30,
+    ("x", 1, 1, 1, 0): 31,
+    ("x", -1, 2, 0, 1): 32,
+    ("xl", 0): 33,
+    ("z", 1, 3, 0, 0): 34,
+    ("b", (-2, 0), 0): 35,
+    ("cw", 0): 36,
+    ("x", -1, 1, 1, 1): 37,
+    ("y", -2, 0): 38,
     ("x", 1, 1, 1, 1): 39,
-    ("cw", 0): 40,
-    ("z", 1, 3, 0, 64): 41,
-    ("z", -1, 3, 0, 64): 42,
-    ("p", (3, 0), 0): 43,
-    ("y", 2, 0): 44,
-    ("zo", 1): 45,
-    ("c", (2, 0), 0): 46,
-    ("z", 1, 4, 0, 0): 47,
-    ("c", (0, 1), 0): 48,
-    ("b", (3, 0), 0): 49,
-    ("z", -1, 1, 1, 0): 50,
+    ("z", -1, 3, 0, 64): 40,
+    ("b", (0, 1), 0): 41,
+    ("z", -1, 3, 0, 0): 42,
+    ("y", 2, 0): 43,
+    ("p", (3, 0), 0): 44,
+    ("zo", 0): 45,
+    ("zo", 1): 46,
+    ("c", (2, 0), 0): 47,
+    ("b", (3, 0), 0): 48,
+    ("z", 1, 3, 0, 64): 49,
+    ("p", (-3, 0), 0): 50,
     ("c", (1, 0), 0): 51,
-    ("c", (-2, 0), 0): 52,
-    ("b", (-3, 0), 0): 53,
-    ("y", -2, 1): 54,
-    ("c", (-1, 0), 0): 55,
-    ("d", (0, 0), 0): 56,
+    ("c", (0, 1), 0): 52,
+    ("z", 1, 4, 0, 0): 53,
+    ("b", (-3, 0), 0): 54,
+    ("y", -2, 1): 55,
+    ("p", (-2, 1), 0): 56,
     ("x", 1, 2, 1, 0): 57,
-    ("x", -1, 2, 1, 1): 58,
-    ("xl", 1): 59,
-    ("z", 1, 1, 1, 0): 60,
-    ("cw", 1): 61,
-    ("z", -1, 4, 0, 64): 62,
-    ("p", (4, 0), 0): 63,
-    ("d", (2, 0), 0): 64,
-    ("y", 2, 1): 65,
-    ("p", (2, 1), 0): 66,
-    ("p", (1, 1), 0): 67,
-    ("d", (-1, 0), 0): 68,
-    ("b", (2, 1), 0): 69,
-    ("b", (4, 0), 0): 70,
-    ("wg", 0): 71,
-    ("b", (1, 1), 0): 72,
-    ("d", (0, 1), 0): 73,
-    ("c", (-3, 0), 0): 74,
-    ("d", (1, 0), 0): 75,
-    ("c", (3, 0), 0): 76,
-    ("z", 1, 3, 1, 0): 77,
-    ("z", -1, 3, 1, 0): 78,
-    ("y", 4, 0): 79,
-    ("p", (3, 1), 0): 80,
-    ("d", (-2, 0), 0): 81,
-    ("b", (-2, 1), 0): 82,
-    ("b", (-1, 1), 0): 83,
-    ("p", (4, 1), 0): 84,
-    ("wg", 2): 85,
-    ("c", (1, 1), 0): 86,
-    ("b", (3, 1), 0): 87,
-    ("b", (4, 1), 0): 88,
-    ("wg", 1): 89,
-    ("z", -1, 1, 1, 64): 90,
-    ("b", (-3, 1), 0): 91,
-    ("z", 1, 1, 1, 64): 92,
-    ("p", (1, 1), 64): 93,
-    ("wg", 3): 94,
-    ("c", (4, 0), 0): 95,
-    ("z", -1, 3, 1, 64): 96,
-    ("z", 1, 3, 1, 64): 97,
-    ("b", (1, 1), 64): 98,
-    ("y", 4, 1): 99,
-    ("p", (4, 1), 64): 100,
-    ("d", (-3, 0), 0): 101,
-    ("p", (3, 1), 64): 102,
-    ("c", (-1, 1), 0): 103,
-    ("b", (4, 1), 64): 104,
-    ("c", (-3, 1), 0): 105,
-    ("b", (-1, 1), 64): 106,
-    ("c", (3, 1), 0): 107,
-    ("d", (3, 0), 0): 108,
+    ("z", -1, 4, 0, 64): 58,
+    ("p", (4, 0), 0): 59,
+    ("d", (0, 0), 0): 60,
+    ("c", (-2, 0), 0): 61,
+    ("c", (-1, 0), 0): 62,
+    ("b", (-2, 1), 0): 63,
+    ("x", -1, 2, 1, 1): 64,
+    ("xl", 1): 65,
+    ("wg", 0): 66,
+    ("d", (2, 0), 0): 67,
+    ("cw", 1): 68,
+    ("y", 2, 1): 69,
+    ("p", (2, 1), 0): 70,
+    ("b", (4, 0), 0): 71,
+    ("d", (1, 0), 0): 72,
+    ("z", 1, 3, 1, 0): 73,
+    ("wg", 1): 74,
+    ("z", -1, 3, 1, 0): 75,
+    ("p", (3, 1), 0): 76,
+    ("y", 4, 0): 77,
+    ("c", (-2, 1), 0): 78,
+    ("c", (-3, 0), 0): 79,
+    ("c", (3, 0), 0): 80,
+    ("wg", 2): 81,
+    ("d", (-1, 0), 0): 82,
+    ("z", 1, 1, 1, 0): 83,
+    ("b", (2, 1), 0): 84,
+    ("b", (3, 1), 0): 85,
+    ("z", -1, 1, 1, 0): 86,
+    ("wg", 4): 87,
+    ("b", (-3, 1), 0): 88,
+    ("c", (4, 0), 0): 89,
+    ("d", (-2, 0), 0): 90,
+    ("p", (1, 1), 0): 91,
+    ("wg", 3): 92,
+    ("y", 4, 1): 93,
+    ("p", (4, 1), 0): 94,
+    ("z", 1, 1, 1, 64): 95,
+    ("b", (1, 1), 0): 96,
+    ("b", (-1, 1), 0): 97,
+    ("d", (-3, 0), 0): 98,
+    ("wg", 6): 99,
+    ("d", (3, 0), 0): 100,
+    ("z", 1, 3, 1, 64): 101,
+    ("c", (2, 1), 0): 102,
+    ("z", -1, 1, 1, 64): 103,
+    ("p", (1, 1), 64): 104,
+    ("c", (3, 1), 0): 105,
+    ("d", (4, 0), 0): 106,
+    ("b", (4, 1), 0): 107,
+    ("d", (-2, 1), 0): 108,
     ("z", 1, 3, 1, 96): 109,
-    ("z", -1, 3, 1, 96): 110,
-    ("wg", 4): 111,
-    ("c", (2, 1), 0): 112,
-    ("b", (3, 1), 64): 113,
-    ("p", (3, 1), 96): 114,
-    ("b", (-3, 1), 64): 115,
-    ("c", (4, 1), 0): 116,
-    ("wg", 5): 117,
-    ("d", (1, 1), 0): 118,
-    ("b", (3, 1), 96): 119,
-    ("b", (-3, 1), 96): 120,
-    ("c", (-2, 1), 0): 121,
+    ("b", (4, 1), 64): 110,
+    ("wg", 5): 111,
+    ("b", (1, 1), 64): 112,
+    ("c", (-3, 1), 0): 113,
+    ("z", -1, 3, 1, 64): 114,
+    ("c", (1, 1), 0): 115,
+    ("c", (-1, 1), 0): 116,
+    ("d", (0, 1), 0): 117,
+    ("b", (-1, 1), 64): 118,
+    ("z", -1, 3, 1, 96): 119,
+    ("p", (3, 1), 64): 120,
+    ("wg", 7): 121,
     ("d", (2, 1), 0): 122,
-    ("c", (1, 1), 64): 123,
-    ("c", (-1, 1), 64): 124,
-    ("d", (-1, 1), 0): 125,
-    ("d", (4, 0), 0): 126,
-    ("d", (-3, 1), 0): 127,
-    ("c", (4, 1), 64): 128,
-    ("wg", 7): 129,
-    ("c", (3, 1), 64): 130,
-    ("d", (3, 1), 0): 131,
-    ("d", (4, 1), 0): 132,
-    ("c", (-3, 1), 64): 133,
-    ("c", (-3, 1), 96): 134,
-    ("c", (3, 1), 96): 135,
-    ("d", (1, 1), 64): 136,
+    ("c", (4, 1), 0): 123,
+    ("b", (3, 1), 64): 124,
+    ("b", (3, 1), 96): 125,
+    ("d", (3, 1), 0): 126,
+    ("b", (-3, 1), 64): 127,
+    ("b", (-3, 1), 96): 128,
+    ("c", (4, 1), 64): 129,
+    ("c", (1, 1), 64): 130,
+    ("c", (-1, 1), 64): 131,
+    ("d", (-3, 1), 0): 132,
+    ("d", (-1, 1), 0): 133,
+    ("d", (1, 1), 0): 134,
+    "out": 135,
+    ("d", (4, 1), 0): 136,
     ("d", (-1, 1), 64): 137,
-    ("d", (-2, 1), 0): 138,
-    ("d", (-3, 1), 64): 139,
-    ("wg", 6): 140,
-    ("d", (4, 1), 64): 141,
-    ("d", (3, 1), 64): 142,
-    ("d", (3, 1), 96): 143,
-    ("d", (-3, 1), 96): 144,
-    ("e", 0): 145,
-    "out": 146,
-    ("e", 64): 147,
-    ("e", 96): 148,
-    "end": 149,
+    ("c", (3, 1), 64): 138,
+    ("d", (1, 1), 64): 139,
+    ("c", (-3, 1), 64): 140,
+    ("c", (3, 1), 96): 141,
+    ("c", (-3, 1), 96): 142,
+    ("d", (-3, 1), 96): 143,
+    ("e", 0): 144,
+    ("d", (4, 1), 64): 145,
+    ("d", (-3, 1), 64): 146,
+    ("d", (3, 1), 96): 147,
+    ("d", (3, 1), 64): 148,
+    ("e", 96): 149,
+    ("e", 64): 150,
+    "end": 151,
 }
 
 
@@ -199,7 +207,7 @@
 
 def kernel(
     in_hbm, og_hbm, w_hbm, ig_hbm, wg_hbm,
-    og, inp, w, w_hi, w_lo, part, from_core, from_up, from_down, from_y, wg, v_hi, v_lo,
+    og, inp, w, w_hi, w_lo, part, from_core, from_up, from_down, from_y, wg,
     local_sem, send_sem, recv_sem,
 ):
     rows, width = in_hbm.shape
@@ -271,9 +279,8 @@
         return remote(("c", s, xrel % 4), src, dst, sibling)
 
     def send(copy_of, *key):
-        copy = copy_of(*key, False)
-        copy.start()
-        sent.append((None, copy))
+        copy_of(*key, False).start()
+        sent.append(lambda: (None, [copy_of(*key, False)]))
 
     def receive(copy_of, *key):
         copy_of(*key, True).wait_recv()
@@ -310,28 +317,25 @@
         cut = pl.ds(lo, n)
         return remote(("r", lo), part.at[slot(b), cut], from_y.at[cut], y_near)
 
-    def send_when(cond, copies):
+    def send_when(make):
+        cond, copies = make()
+
         @pl.when(cond)
         def _():
             for copy in copies:
                 copy.start()
 
-        sent.append((cond, copies))
-
-    def partial(blocks, lo, n):
-        m = len(blocks) * n
-        value = jnp.concatenate([og[og_at(*b), lo : lo + n] for b in blocks], 0)
-        v_hi[:m], v_lo[:m] = split(value)
-
-        @pl.loop(0, width // 256)
-        def _(i):
-            cut = pl.ds(pl.multiple_of(i * 256, 256), 256)
-            sums = dot3((v_hi[:m], v_lo[:m]), (w_hi[cut], w_lo[cut]), ((1,), (1,)))
-            for k, b in enumerate(blocks):
-                part[slot(b), lo : lo + n, cut] = sums[k * n : (k + 1) * n]
-
-        for b in blocks:
-            send_when(jnp.logical_not(mine(b)), [p_copy(b, lo, n)])
+        sent.append(make)
+
+    def partial_sends(sends):
+        for b, lo, n in sends:
+            send_when(lambda b=b, lo=lo, n=n: (jnp.logical_not(mine(b)), [p_copy(b, lo, n)]))
+
+    def partial(halves):
+        value = jnp.concatenate([og[t, pl.ds(lo, half)] for t, _, lo in halves], 0)
+        sums = dot3(split(value), (w_hi[...], w_lo[...]), ((1,), (0,)))
+        for i, (_, k, lo) in enumerate(halves):
+            part[k, pl.ds(lo, half)] = sums[i * half : (i + 1) * half]
 
     def rs_b(blocks, lo, n):
         hn = n // 2
@@ -341,10 +345,18 @@
                 p_copy(b, lo, n).wait_recv()
                 part[slot(b), lo : lo + n] += from_core[b[0] % 8, lo : lo + n]
 
-            at = from_root(b)
-            send_when(mine(b) & (at == 2), [tree_copy(-1, b, lo, hn), tree_copy(1, b, lo + hn, hn)])
-            send_when(mine(b) & (at == 1), [tree_copy(-1, b, lo + hn, hn)])
-            send_when(mine(b) & (at == 3), [tree_copy(1, b, lo, hn)])
+            def place(at, b=b):
+                return mine(b) & (from_root(b) == at)
+
+            def down(ch, b=b):
+                return tree_copy(-1, b, lo + ch * hn, hn)
+
+            def up(ch, b=b):
+                return tree_copy(1, b, lo + ch * hn, hn)
+
+            send_when(lambda place=place, down=down, up=up: (place(2), [down(0), up(1)]))
+            send_when(lambda place=place, down=down: (place(1), [down(1)]))
+            send_when(lambda place=place, up=up: (place(3), [up(0)]))
 
     def rs_c(blocks, lo, n):
         hn = n // 2
@@ -359,7 +371,12 @@
                     tree_copy(way, b, lo_, hn).wait_recv()
                     part[slot(b), lo_ : lo_ + hn] += landing[b[0] % 8, lo_ : lo_ + hn]
 
-                send_when(cond, [tree_copy(way, b, lo_, hn)])
+                send_when(
+                    lambda b=b, place=place, way=way, lo_=lo_: (
+                        mine(b) & (from_root(b) == place),
+                        [tree_copy(way, b, lo_, hn)],
+                    )
+                )
 
     def rs_d(blocks, lo, n):
         hn = n // 2
@@ -377,8 +394,10 @@
                 )
 
             send_when(
-                cond & (root_y(b) != yl),
-                [root_copy(b, *p) for p in PIECES if lo <= p[0] < lo + n],
+                lambda b=b: (
+                    mine(b) & (from_root(b) == 0) & (root_y(b) != yl),
+                    [root_copy(b, *p) for p in PIECES if lo <= p[0] < lo + n],
+                )
             )
 
     own_slot = (col - z + 8) % 8 * 2 + (c + h) % 2
@@ -394,15 +413,10 @@
         part[own_slot, lo : lo + n] += from_y[lo : lo + n]
         own_out(lo, n).start()
 
-    def weight_sum(places, first):
-        v_hi[...], v_lo[...] = split(jnp.concatenate([og[t] for t in places], 0))
-
-        @pl.loop(0, width // 256)
-        def _(i):
-            cut = pl.ds(pl.multiple_of(i * 256, 256), 256)
-            left = jnp.concatenate([inp[t, :, cut] for t in places], 0).T
-            sums = dot3(split(left), (v_hi[...], v_lo[...]), ((1,), (0,)))
-            wg[cut] = sums if first else wg[cut] + sums
+    def weight_sum(places):
+        left = jnp.concatenate([inp[t] for t in places], 0).T
+        right = jnp.concatenate([og[t] for t in places], 0)
+        wg[...] += dot3(split(left), split(right), ((1,), (0,)))
 
     both = (1, -1)
 
@@ -432,7 +446,8 @@
         send(c_copy, 0, 0)
         own_og.wait()
         own_w.wait()
-        w_hi[...], w_lo[...] = split(w[...])
+        w_hi[...], w_lo[...] = split(w[...].T)
+        wg[...] = jnp.zeros_like(wg)
         own_in.wait()
 
     def y_send():
@@ -506,28 +521,65 @@
     at(("xl", 1), x_last, 1)
     for s in (0, 1):
         at(("cw", s), c_wait, s)
-    for blocks, pieces in GROUPS:
-        for lo, n in pieces:
-            at(("p", blocks[0], lo), partial, blocks, lo, n)
-            for b in blocks:
-                at(("b", b, lo), rs_b, [b], lo, n)
-                at(("c", b, lo), rs_c, [b], lo, n)
-                at(("d", b, lo), rs_d, [b], lo, n)
+    for key, halves, sends in partial_steps():
+        at(key, None, [(og_at(*b), slot(b), lo) for b, lo in halves], sends)
+    for b in [(zrel, s) for zrel in ORDER for s in (0, 1)]:
+        for lo, n in pieces_of(b):
+            at(("b", b, lo), rs_b, [b], lo, n)
+            at(("c", b, lo), rs_c, [b], lo, n)
+            at(("d", b, lo), rs_d, [b], lo, n)
     for i in range(4):
         places = [col_of(i // 2, i % 2 * 2 + k) * 2 + h for k in (0, 1)]
-        at(("wg", i), weight_sum, places, i == 0)
+        at(("wg", i), None, places, None)
     for i, blocks in enumerate(PAIRS):
-        at(("wg", 4 + i), weight_sum, [og_at(*b) for b in blocks], False)
+        at(("wg", 4 + i), None, [og_at(*b) for b in blocks], None)
     out = pltpu.make_async_copy(wg, wg_hbm, local_sem.at[0])
     at("out", out.start)
     at("end", out.wait)
+    passes = [[]]
+    dots = []
     for _, _, key, step, args in sorted(steps, key=lambda e: e[:2]):
+        if step is not None:
+            passes[-1].append((step, args))
+            continue
+        dots.append(args[0])
+        passes.append([] if args[1] is None else [(partial_sends, (args[1],))])
+
+    def pick(i, values):
+        out = values[0]
+        for k, value in enumerate(values[1:], 1):
+            out = jnp.where(i == k, value, out)
+        return out
+
+    @pl.loop(0, len(dots))
+    def _(i):
+        for k in range(len(dots)):
+            @pl.when(i == k)
+            def _():
+                for step, args in passes[k]:
+                    step(*args)
+
+        is_partial = [isinstance(d[0], tuple) for d in dots]
+        flat = [[d[0] if p else (d[0], 0, 0), d[1] if p else (d[1], 0, 0)] for d, p in zip(dots, is_partial, strict=True)]
+        args = [[pick(i, [d[e][f] for d in flat]) for f in range(3)] for e in (0, 1)]
+        sums_here = pick(i, [int(p) for p in is_partial]) == 1
+
+        @pl.when(sums_here)
+        def _():
+            partial([(t, k, pl.multiple_of(lo, half)) for t, k, lo in args])
+
+        @pl.when(jnp.logical_not(sums_here))
+        def _():
+            weight_sum([t for t, _, _ in args])
+
+    for step, args in passes[-1]:
         step(*args)
     for lo, n in PIECES:
         own_out(lo, n).wait()
-    for cond, copies in sent:
+    for make in sent:
+        cond, copies = make()
         if cond is None:
-            copies.wait_send()
+            copies[0].wait_send()
         else:
             @pl.when(cond)
             def _():
@@ -577,8 +629,6 @@
                 vmem((8, rows, features), F32),
                 vmem((rows, features), F32),
                 vmem(weight.shape, F32),
-                vmem((2 * rows, width), BF16),
-                vmem((2 * rows, width), BF16),
                 dma((8,)),
                 dma((N_SEM,)),
                 dma((N_SEM,)),

time: 90.1 us -> 82.3 us (0.913)
  Pallas kernels: 88.4 us -> 81.5 us
    pallas_call x1, Pallas kernels: 85.7 us -> 78.8 us  [local(): pl.pallas_call(kernel, out_shape=sums_shape, in_specs=[pl.BlockSpec(memor...]
where the time goes in v4:
time: 82.3 us; the launch traced here: 82.1 us
  Pallas kernels  81.5 us (99%)
    pallas_call x1, Pallas kernels, local(): pl.pallas_call(kernel, out_shape=sums_shape, in_specs=[pl.BlockSpec(memor...  78.8 us
    pallas_call x1, Pallas kernels, local(): pl.pallas_call(move, out_shape=sums_shape, in_specs=[pl.BlockSpec(memory_...  2.67 us

profile of v4, /device:TPU:22, one launch (start us, length us, event | category | flops | bytes accessed | tf_op | source)
XLA Modules:
  0.0 82.1 jit_solution(14547472935624519677)
XLA Ops:
  0.6 78.8 %shard_map.50 = (f32[128,768]{1,0:T(8,128)}, f32[768,768]{1,0:T(8,128)}) custom-call(f32[128,768]{1,0:T(8,128)} %in_hbm.1, f32[128,768]{1,0:T(8,128)} %og_hbm.1, f32[768,768]{1,0:T(8,128)} %w_hbm.1), custom_call_target="tpu_custom_call" | custom-call | tf_op jit(solution)/shard_map/pallas_call | solution.py:615
  79.5 2.7 %shard_map.51 = (f32[128,768]{1,0:T(8,128)}, f32[768,768]{1,0:T(8,128)}) custom-call(f32[128,768]{1,0:T(8,128)} %get-tuple-element.4.ig_in, f32[768,768]{1,0:T(8,128)} %get-tuple-element.5.wg_in), custom_call_target="tpu_custom_call" | custom-call | tf_op jit(solution)/shard_map/pallas_call | solution.py:642

commit v5 on v4

--- a/solution.py
+++ b/solution.py
@@ -41,8 +41,8 @@
     "begin": 0,
     "ysend": 1,
     ("p", (0, 0), 0): 2,
-    ("z", 1, 1, 0, 0): 3,
-    ("b", (0, 0), 0): 4,
+    ("b", (0, 0), 0): 3,
+    ("z", 1, 1, 0, 0): 4,
     ("z", -1, 1, 0, 0): 5,
     ("x", 1, 1, 0, 0): 6,
     ("x", -1, 1, 0, 0): 7,
@@ -51,144 +51,144 @@
     ("x", 1, 1, 0, 1): 10,
     ("x", -1, 1, 0, 1): 11,
     ("l", 1): 12,
-    ("p", (1, 0), 0): 13,
-    ("z", 1, 1, 0, 64): 14,
-    ("p", (-1, 0), 0): 15,
-    ("b", (1, 0), 0): 16,
-    ("z", 1, 2, 0, 0): 17,
-    ("c", (0, 0), 0): 18,
-    ("b", (-1, 0), 0): 19,
-    ("z", -1, 2, 0, 0): 20,
-    ("y", 0, 0): 21,
-    ("x", 1, 2, 0, 0): 22,
-    ("x", -1, 1, 1, 0): 23,
-    ("z", 1, 2, 0, 64): 24,
-    ("p", (-2, 0), 0): 25,
-    ("z", -1, 2, 0, 64): 26,
-    ("p", (2, 0), 0): 27,
-    ("b", (2, 0), 0): 28,
-    ("y", 0, 1): 29,
-    ("p", (0, 1), 0): 30,
-    ("x", 1, 1, 1, 0): 31,
-    ("x", -1, 2, 0, 1): 32,
-    ("xl", 0): 33,
-    ("z", 1, 3, 0, 0): 34,
-    ("b", (-2, 0), 0): 35,
+    ("z", 1, 1, 0, 64): 13,
+    ("p", (-1, 0), 0): 14,
+    ("z", 1, 2, 0, 0): 15,
+    ("y", 0, 0): 16,
+    ("z", -1, 2, 0, 0): 17,
+    ("x", 1, 2, 0, 0): 18,
+    ("p", (1, 0), 0): 19,
+    ("z", 1, 2, 0, 64): 20,
+    ("x", -1, 1, 1, 0): 21,
+    ("b", (-1, 0), 0): 22,
+    ("b", (1, 0), 0): 23,
+    ("y", 0, 1): 24,
+    ("z", -1, 2, 0, 64): 25,
+    ("p", (2, 0), 0): 26,
+    ("b", (2, 0), 0): 27,
+    ("p", (0, 1), 0): 28,
+    ("x", 1, 1, 1, 0): 29,
+    ("x", -1, 2, 0, 1): 30,
+    ("xl", 0): 31,
+    ("p", (-2, 0), 0): 32,
+    ("b", (-2, 0), 0): 33,
+    ("c", (0, 0), 0): 34,
+    ("z", 1, 3, 0, 0): 35,
     ("cw", 0): 36,
-    ("x", -1, 1, 1, 1): 37,
-    ("y", -2, 0): 38,
-    ("x", 1, 1, 1, 1): 39,
-    ("z", -1, 3, 0, 64): 40,
-    ("b", (0, 1), 0): 41,
-    ("z", -1, 3, 0, 0): 42,
-    ("y", 2, 0): 43,
-    ("p", (3, 0), 0): 44,
-    ("zo", 0): 45,
-    ("zo", 1): 46,
-    ("c", (2, 0), 0): 47,
-    ("b", (3, 0), 0): 48,
-    ("z", 1, 3, 0, 64): 49,
-    ("p", (-3, 0), 0): 50,
+    ("y", -2, 0): 37,
+    ("x", 1, 1, 1, 1): 38,
+    ("x", -1, 1, 1, 1): 39,
+    ("b", (0, 1), 0): 40,
+    ("z", -1, 3, 0, 0): 41,
+    ("z", -1, 3, 0, 64): 42,
+    ("c", (2, 0), 0): 43,
+    ("y", 2, 0): 44,
+    ("p", (3, 0), 0): 45,
+    ("zo", 0): 46,
+    ("zo", 1): 47,
+    ("z", 1, 3, 0, 64): 48,
+    ("p", (-3, 0), 0): 49,
+    ("z", 1, 4, 0, 0): 50,
     ("c", (1, 0), 0): 51,
-    ("c", (0, 1), 0): 52,
-    ("z", 1, 4, 0, 0): 53,
-    ("b", (-3, 0), 0): 54,
-    ("y", -2, 1): 55,
-    ("p", (-2, 1), 0): 56,
-    ("x", 1, 2, 1, 0): 57,
-    ("z", -1, 4, 0, 64): 58,
-    ("p", (4, 0), 0): 59,
+    ("b", (-3, 0), 0): 52,
+    ("y", -2, 1): 53,
+    ("p", (-2, 1), 0): 54,
+    ("b", (3, 0), 0): 55,
+    ("x", 1, 2, 1, 0): 56,
+    ("z", -1, 4, 0, 64): 57,
+    ("p", (4, 0), 0): 58,
+    ("c", (-2, 0), 0): 59,
     ("d", (0, 0), 0): 60,
-    ("c", (-2, 0), 0): 61,
-    ("c", (-1, 0), 0): 62,
-    ("b", (-2, 1), 0): 63,
-    ("x", -1, 2, 1, 1): 64,
-    ("xl", 1): 65,
-    ("wg", 0): 66,
-    ("d", (2, 0), 0): 67,
-    ("cw", 1): 68,
-    ("y", 2, 1): 69,
-    ("p", (2, 1), 0): 70,
-    ("b", (4, 0), 0): 71,
-    ("d", (1, 0), 0): 72,
-    ("z", 1, 3, 1, 0): 73,
+    ("b", (-2, 1), 0): 61,
+    ("x", -1, 2, 1, 1): 62,
+    ("xl", 1): 63,
+    ("wg", 0): 64,
+    ("y", 2, 1): 65,
+    ("z", 1, 3, 1, 0): 66,
+    ("c", (-1, 0), 0): 67,
+    ("d", (2, 0), 0): 68,
+    ("p", (2, 1), 0): 69,
+    ("cw", 1): 70,
+    ("d", (1, 0), 0): 71,
+    ("b", (4, 0), 0): 72,
+    ("z", -1, 3, 1, 0): 73,
     ("wg", 1): 74,
-    ("z", -1, 3, 1, 0): 75,
-    ("p", (3, 1), 0): 76,
-    ("y", 4, 0): 77,
-    ("c", (-2, 1), 0): 78,
-    ("c", (-3, 0), 0): 79,
-    ("c", (3, 0), 0): 80,
-    ("wg", 2): 81,
-    ("d", (-1, 0), 0): 82,
-    ("z", 1, 1, 1, 0): 83,
+    ("c", (0, 1), 0): 75,
+    ("c", (3, 0), 0): 76,
+    ("p", (3, 1), 0): 77,
+    ("z", 1, 1, 1, 0): 78,
+    ("y", 4, 0): 79,
+    ("c", (-2, 1), 0): 80,
+    ("c", (-3, 0), 0): 81,
+    ("wg", 2): 82,
+    ("wg", 4): 83,
     ("b", (2, 1), 0): 84,
-    ("b", (3, 1), 0): 85,
-    ("z", -1, 1, 1, 0): 86,
-    ("wg", 4): 87,
-    ("b", (-3, 1), 0): 88,
+    ("d", (-1, 0), 0): 85,
+    ("b", (3, 1), 0): 86,
+    ("b", (-3, 1), 0): 87,
+    ("z", -1, 1, 1, 0): 88,
     ("c", (4, 0), 0): 89,
     ("d", (-2, 0), 0): 90,
     ("p", (1, 1), 0): 91,
     ("wg", 3): 92,
-    ("y", 4, 1): 93,
-    ("p", (4, 1), 0): 94,
-    ("z", 1, 1, 1, 64): 95,
-    ("b", (1, 1), 0): 96,
-    ("b", (-1, 1), 0): 97,
-    ("d", (-3, 0), 0): 98,
+    ("d", (-3, 0), 0): 93,
+    ("z", 1, 1, 1, 64): 94,
+    ("y", 4, 1): 95,
+    ("p", (4, 1), 0): 96,
+    ("b", (1, 1), 0): 97,
+    ("b", (-1, 1), 0): 98,
     ("wg", 6): 99,
     ("d", (3, 0), 0): 100,
-    ("z", 1, 3, 1, 64): 101,
-    ("c", (2, 1), 0): 102,
-    ("z", -1, 1, 1, 64): 103,
-    ("p", (1, 1), 64): 104,
-    ("c", (3, 1), 0): 105,
-    ("d", (4, 0), 0): 106,
-    ("b", (4, 1), 0): 107,
-    ("d", (-2, 1), 0): 108,
-    ("z", 1, 3, 1, 96): 109,
-    ("b", (4, 1), 64): 110,
+    ("b", (4, 1), 0): 101,
+    ("z", 1, 3, 1, 64): 102,
+    ("c", (2, 1), 0): 103,
+    ("z", -1, 1, 1, 64): 104,
+    ("p", (1, 1), 64): 105,
+    ("d", (0, 1), 0): 106,
+    ("c", (3, 1), 0): 107,
+    ("d", (4, 0), 0): 108,
+    ("b", (4, 1), 64): 109,
+    ("d", (-2, 1), 0): 110,
     ("wg", 5): 111,
     ("b", (1, 1), 64): 112,
-    ("c", (-3, 1), 0): 113,
-    ("z", -1, 3, 1, 64): 114,
-    ("c", (1, 1), 0): 115,
-    ("c", (-1, 1), 0): 116,
-    ("d", (0, 1), 0): 117,
-    ("b", (-1, 1), 64): 118,
-    ("z", -1, 3, 1, 96): 119,
-    ("p", (3, 1), 64): 120,
-    ("wg", 7): 121,
+    ("c", (1, 1), 0): 113,
+    ("c", (-1, 1), 0): 114,
+    ("z", 1, 3, 1, 96): 115,
+    ("b", (-1, 1), 64): 116,
+    ("z", -1, 3, 1, 64): 117,
+    ("z", -1, 3, 1, 96): 118,
+    ("p", (3, 1), 64): 119,
+    ("c", (4, 1), 0): 120,
+    ("c", (-3, 1), 0): 121,
     ("d", (2, 1), 0): 122,
-    ("c", (4, 1), 0): 123,
+    ("b", (-3, 1), 64): 123,
     ("b", (3, 1), 64): 124,
     ("b", (3, 1), 96): 125,
     ("d", (3, 1), 0): 126,
-    ("b", (-3, 1), 64): 127,
-    ("b", (-3, 1), 96): 128,
-    ("c", (4, 1), 64): 129,
-    ("c", (1, 1), 64): 130,
-    ("c", (-1, 1), 64): 131,
-    ("d", (-3, 1), 0): 132,
-    ("d", (-1, 1), 0): 133,
+    ("b", (-3, 1), 96): 127,
+    ("c", (4, 1), 64): 128,
+    ("c", (-1, 1), 64): 129,
+    ("d", (-1, 1), 0): 130,
+    ("c", (1, 1), 64): 131,
+    ("wg", 7): 132,
+    "out": 133,
     ("d", (1, 1), 0): 134,
-    "out": 135,
-    ("d", (4, 1), 0): 136,
-    ("d", (-1, 1), 64): 137,
-    ("c", (3, 1), 64): 138,
-    ("d", (1, 1), 64): 139,
+    ("d", (-3, 1), 0): 135,
+    ("d", (-1, 1), 64): 136,
+    ("d", (1, 1), 64): 137,
+    ("d", (4, 1), 0): 138,
+    ("c", (3, 1), 64): 139,
     ("c", (-3, 1), 64): 140,
-    ("c", (3, 1), 96): 141,
-    ("c", (-3, 1), 96): 142,
-    ("d", (-3, 1), 96): 143,
-    ("e", 0): 144,
-    ("d", (4, 1), 64): 145,
-    ("d", (-3, 1), 64): 146,
+    ("d", (-3, 1), 64): 141,
+    ("d", (3, 1), 64): 142,
+    ("c", (3, 1), 96): 143,
+    ("c", (-3, 1), 96): 144,
+    ("d", (-3, 1), 96): 145,
+    ("e", 0): 146,
     ("d", (3, 1), 96): 147,
-    ("d", (3, 1), 64): 148,
-    ("e", 96): 149,
-    ("e", 64): 150,
+    ("d", (4, 1), 64): 148,
+    ("e", 64): 149,
+    ("e", 96): 150,
     "end": 151,
 }
 

time: 82.3 us -> 80.5 us (0.978)
  Pallas kernels: 81.5 us -> 79.7 us
    pallas_call x1, Pallas kernels: 78.8 us -> 77.1 us  [local(): pl.pallas_call(kernel, out_shape=sums_shape, in_specs=[pl.BlockSpec(memor...]
where the time goes in v5:
time: 80.5 us; the launch traced here: 80.4 us
  Pallas kernels  79.7 us (99%)
    pallas_call x1, Pallas kernels, local(): pl.pallas_call(kernel, out_shape=sums_shape, in_specs=[pl.BlockSpec(memor...  77.1 us
    pallas_call x1, Pallas kernels, local(): pl.pallas_call(move, out_shape=sums_shape, in_specs=[pl.BlockSpec(memory_...  2.67 us

profile of v5, /device:TPU:22, one launch (start us, length us, event | category | flops | bytes accessed | tf_op | source)
XLA Modules:
  0.0 80.4 jit_solution(5055388991259204299)
XLA Ops:
  0.6 77.1 %shard_map.50 = (f32[128,768]{1,0:T(8,128)}, f32[768,768]{1,0:T(8,128)}) custom-call(f32[128,768]{1,0:T(8,128)} %in_hbm.1, f32[128,768]{1,0:T(8,128)} %og_hbm.1, f32[768,768]{1,0:T(8,128)} %w_hbm.1), custom_call_target="tpu_custom_call" | custom-call | tf_op jit(solution)/shard_map/pallas_call | solution.py:615
  77.7 2.7 %shard_map.51 = (f32[128,768]{1,0:T(8,128)}, f32[768,768]{1,0:T(8,128)}) custom-call(f32[128,768]{1,0:T(8,128)} %get-tuple-element.4.ig_in, f32[768,768]{1,0:T(8,128)} %get-tuple-element.5.wg_in), custom_call_target="tpu_custom_call" | custom-call | tf_op jit(solution)/shard_map/pallas_call | solution.py:642

commit v6 on v5

--- a/solution.py
+++ b/solution.py
@@ -95,9 +95,9 @@
     ("p", (-2, 1), 0): 54,
     ("b", (3, 0), 0): 55,
     ("x", 1, 2, 1, 0): 56,
-    ("z", -1, 4, 0, 64): 57,
-    ("p", (4, 0), 0): 58,
-    ("c", (-2, 0), 0): 59,
+    ("c", (-2, 0), 0): 57,
+    ("z", -1, 4, 0, 64): 58,
+    ("p", (4, 0), 0): 59,
     ("d", (0, 0), 0): 60,
     ("b", (-2, 1), 0): 61,
     ("x", -1, 2, 1, 1): 62,
@@ -116,11 +116,11 @@
     ("c", (0, 1), 0): 75,
     ("c", (3, 0), 0): 76,
     ("p", (3, 1), 0): 77,
-    ("z", 1, 1, 1, 0): 78,
-    ("y", 4, 0): 79,
-    ("c", (-2, 1), 0): 80,
-    ("c", (-3, 0), 0): 81,
-    ("wg", 2): 82,
+    ("y", 4, 0): 78,
+    ("c", (-2, 1), 0): 79,
+    ("c", (-3, 0), 0): 80,
+    ("wg", 2): 81,
+    ("z", 1, 1, 1, 0): 82,
     ("wg", 4): 83,
     ("b", (2, 1), 0): 84,
     ("d", (-1, 0), 0): 85,

time: 80.5 us -> 80.5 us (level)
  no operation moved by 1% of the time
where the time goes in v6:
time: 80.5 us; the launch traced here: 80.4 us
  Pallas kernels  79.8 us (99%)
    pallas_call x1, Pallas kernels, local(): pl.pallas_call(kernel, out_shape=sums_shape, in_specs=[pl.BlockSpec(memor...  77.1 us
    pallas_call x1, Pallas kernels, local(): pl.pallas_call(move, out_shape=sums_shape, in_specs=[pl.BlockSpec(memory_...  2.67 us

profile of v6, /device:TPU:22, one launch (start us, length us, event | category | flops | bytes accessed | tf_op | source)
XLA Modules:
  0.0 80.4 jit_solution(11270569617467472)
XLA Ops:
  0.6 77.1 %shard_map.50 = (f32[128,768]{1,0:T(8,128)}, f32[768,768]{1,0:T(8,128)}) custom-call(f32[128,768]{1,0:T(8,128)} %in_hbm.1, f32[128,768]{1,0:T(8,128)} %og_hbm.1, f32[768,768]{1,0:T(8,128)} %w_hbm.1), custom_call_target="tpu_custom_call" | custom-call | tf_op jit(solution)/shard_map/pallas_call | solution.py:615
  77.7 2.7 %shard_map.51 = (f32[128,768]{1,0:T(8,128)}, f32[768,768]{1,0:T(8,128)}) custom-call(f32[128,768]{1,0:T(8,128)} %get-tuple-element.4.ig_in, f32[768,768]{1,0:T(8,128)} %get-tuple-element.5.wg_in), custom_call_target="tpu_custom_call" | custom-call | tf_op jit(solution)/shard_map/pallas_call | solution.py:642
